TPU v7x, 256 devices: a whole 4x4x8 slice. The times are simulated.
256 devices in a mesh: img: 8 (over x, z_hi), ori: 32 (over z_lo, y, core).
Axes of the slice: x: 4, y: 4, z: 8 (z_hi: 2, z_lo: 4; z = z_hi * 4 + z_lo), core: 2. Of those that a mesh axis runs over, the one named last changes fastest.
Arguments:
- images: bfloat16 [1024, 2, 8320], P(('img', 'ori')), may hold values from -60 to 60
- projections: bfloat16 [2048, 2, 8320], P('ori'), may hold values from -6 to 6
- ctf_table: float32 [64, 8320], replicated, may hold values from -1 to 1
- noise_weight: float32 [8320], replicated, may hold values from 0.0039663464 to 0.03966346
- shifts: int32 [1024, 4, 2], P(('img', 'ori')), may hold values from -8 to 8, as said below
- defocus: int32 [1024], P(('img', 'ori')), may hold values from 0 to 63, as said below
Outputs:
- log_evidence: float32 [1024], P(('img', 'ori'))
- class_sums: float32 [2048, 2, 8320], P(('ori', 'img'))
Inputs may be any that keep to these rules, and one draw needn't show every extreme that they name: `shifts`: both ends of the range occur. `defocus`: every class from 0 to 63 may occur; the first and the last do.
All inputs are finite; a program needn't handle non-finite values.
Results may differ from a plain program's by a relative error of at most 0.011.
Values may be sent and summed in bfloat16 or wider, within the bound.
A program may use at most 128 MiB of HBM per device.

v0:
```python
import math

import jax
import jax.numpy as jnp
from jax import lax
from jax.sharding import PartitionSpec as P

KY = 128
KX = 65


TWO_PI = 2.0 * math.pi


def class_lookup(classes, ctf_table):
    labels = jnp.arange(ctf_table.shape[0], dtype=jnp.int32)
    onehot = (classes[:, None] == labels[None, :]).astype(jnp.float32)
    rows_ctf = jnp.dot(
        onehot, ctf_table, precision=lax.Precision.HIGHEST, preferred_element_type=jnp.float32
    )
    return (onehot, rows_ctf)


def shifted_weighted(block, offsets, rows_ctf):
    pixel_index = jnp.arange(block.shape[2], dtype=jnp.int32)
    column = pixel_index % KX
    height = pixel_index // KX
    phase_steps = (
        column[None, None, :] * offsets[:, :, 0:1] + height[None, None, :] * offsets[:, :, 1:2]
    ) % KY
    angles = phase_steps.astype(jnp.float32) * (TWO_PI / KY)
    cosine = jnp.cos(angles)
    sine_part = jnp.sin(angles)
    real_part = block[:, 0, :].astype(jnp.float32)[:, None, :]
    imag_part = block[:, 1, :].astype(jnp.float32)[:, None, :]
    shifted = jnp.stack(
        [real_part * cosine + imag_part * sine_part, imag_part * cosine - real_part * sine_part],
        axis=2,
    )
    return (shifted * rows_ctf[:, None, None, :]).astype(jnp.bfloat16)


def per_device(images, projections, ctf_table, noise_weight, shifts, defocus):
    ori_count = lax.axis_size("ori")
    img_count = lax.axis_size("img")
    local_images = images.shape[0]
    local_proj = projections.shape[0]
    pixels = images.shape[2]
    trans_count = shifts.shape[1]
    group_images = local_images * ori_count
    total_proj = local_proj * ori_count
    weighted = (
        (projections.astype(jnp.float32) * noise_weight[None, None, :])
        .astype(jnp.bfloat16)
        .reshape(local_proj, 2 * pixels)
    )
    power = jnp.sum(jnp.square(projections.astype(jnp.float32)), axis=1)
    class_norm = 0.5 * jnp.dot(
        ctf_table * ctf_table * noise_weight[None, :],
        power.T,
        precision=lax.Precision.HIGHEST,
        preferred_element_type=jnp.float32,
    )
    block = lax.all_gather(images, "ori", axis=0, tiled=True)
    offsets = lax.all_gather(shifts, "ori", axis=0, tiled=True)
    classes = lax.all_gather(defocus, "ori", axis=0, tiled=True)
    count = block.shape[0]
    width = math.gcd(count, 32)

    def one_block(inputs):
        part_images, part_offsets, part_classes = inputs
        onehot, rows_ctf = class_lookup(part_classes, ctf_table)
        prepared = shifted_weighted(part_images, part_offsets, rows_ctf).reshape(
            width * trans_count, 2 * pixels
        )
        cross = lax.dot_general(
            prepared, weighted, (((1,), (1,)), ((), ())), preferred_element_type=jnp.float32
        )
        norms = jnp.dot(
            onehot, class_norm, precision=lax.Precision.HIGHEST, preferred_element_type=jnp.float32
        )
        return (cross.reshape(width, trans_count, local_proj) - norms[:, None, :], prepared)

    stacked, translated = lax.map(
        one_block,
        (
            block.reshape(count // width, width, 2, pixels),
            offsets.reshape(count // width, width, trans_count, 2),
            classes.reshape(count // width, width),
        ),
    )
    piece_out = stacked.reshape(count, trans_count, local_proj)
    piece_prepared = translated.reshape(count, trans_count, 2 * pixels)
    local_top = jnp.max(piece_out, axis=(1, 2))
    largest = lax.pmax(local_top, "ori")
    totals = lax.psum(jnp.sum(jnp.exp(piece_out - largest[:, None, None]), axis=(1, 2)), "ori")
    evidence = largest + jnp.log(totals)
    posterior = (jnp.exp(piece_out - evidence[:, None, None]) * total_proj).astype(jnp.bfloat16)
    share_rows = local_proj // img_count
    flat_prepared = piece_prepared.reshape(group_images * trans_count, 2 * pixels)
    chosen = posterior.reshape(group_images * trans_count, share_rows * lax.axis_size("img"))
    class_part = lax.psum_scatter(
        lax.dot_general(
            chosen, flat_prepared, (((0,), (0,)), ((), ())), preferred_element_type=jnp.float32
        ).astype(jnp.bfloat16),
        "img",
        scatter_dimension=0,
        tiled=True,
    ).astype(jnp.float32)
    class_sums = class_part.reshape(-1, 2, pixels)
    evidence_own = lax.dynamic_slice_in_dim(
        evidence, lax.axis_index("ori") * local_images, local_images, 0
    )
    return (evidence_own, class_sums)


def solution(mesh):
    in_specs = (
        P(("img", "ori"), None, None),
        P("ori", None, None),
        P(),
        P(),
        P(("img", "ori"), None, None),
        P(("img", "ori")),
    )
    out_specs = (P(("img", "ori")), P(("ori", "img"), None, None))
    return jax.shard_map(
        per_device, mesh=mesh, in_specs=in_specs, out_specs=out_specs, check_vma=False
    )
```

profile of v0, /device:TPU:1, one launch (start us, length us, event | category | flops | bytes accessed | tf_op | source)
XLA Modules:
  0.0 506.3 jit_solution(11443747925684179504)
XLA Ops:
  8.0 46.9 %all_gather.10 = s32[128,4,2]{1,2,0:T(2,128)S(1)} all-gather(s32[4,4,2]{1,2,0:T(2,128)} %param.12), channel_id=1, replica_groups=mesh['img'=8,'ori'=32] {'ori'}, dimensions={0}, use_global_device_ids=true | all-gather | bytes 4224 | tf_op jit(solution)/shard_map/all_gather | solution.py:65
  57.8 7.0 %all-reduce = s32[128]{0:T(128)S(1)} all-reduce(s32[128]{0:T(128)S(1)} %dynamic-update-slice), channel_id=1, replica_groups=mesh['img'=8,'ori'=32] {'ori'}, use_global_device_ids=true, to_apply=%add | all-reduce | flops 128 | bytes 1024
  64.9 8.9 %fusion.31 = (f32[64,8320]{1,0:T(8,128)S(1)}, bf16[64,2,8320]{2,1,0:T(2,128)(2,1)S(1)}) fusion(bf16[64,2,8320]{2,1,0:T(2,128)(2,1)} %param.9, f32[8320]{0:T(1024)} %param.11), kind=kLoop, calls=%fused_computation.51 | loop fusion | flops 4792320 | bytes 6423040 | tf_op jit(solution)/shard_map/reduce_sum | solution.py:57
  75.3 2.2 fusion.35
  77.7 177.2 %while.15 = (s32[]{:T(128)}, f32[4,32,4,64]{3,1,2,0:T(8,128)S(1)}, bf16[4,128,16640]{2,1,0:T(8,128)(2,1)}, bf16[4,32,2,8320]{3,2,1,0:T(2,128)(2,1)}, s32[4,32,4,...) while((s32[]{:T(128)}, f32[4,32,4,64]{3,1,2,0:T(8,128)S(1)}, ...), condition=%wide.region_2.3_spmd, body=%wide.region_1.2_spmd.sunk | while | flops 513398272 | bytes 128040664 | solution.py:84
  80.0 17.7 %multiply_add_fusion.2 = (f32[32,4,1,8320]{3,0,2,1:T(8,128)S(1)}, f32[32,4,1,8320]{3,0,2,1:T(8,128)S(1)}) fusion(f32[32,8320]{1,0:T(8,128)S(1)} %get-tuple-element.295, s32[32,4]{0,1:T(4,128)S(1)} %get-tuple-element.296, s32[8320]{0:T(1024)S(1)} %get-tuple-element.297, s32[32,4]{0,1:T(4,128)S(1)} %get-tuple-element.298, ...), kind=kLoop, calls=%fused_computation.13.clone.1 | loop fusion | flops 23429120 | bytes 10717184 | tf_op jit(solution)/shard_map/while/body/eval_jaxpr/add | solution.py:37
  100.7 2.1 mul.436
  104.4 5.3 %copy.61 = bf16[32,4,2,8320]{3,2,1,0:T(2,128)(2,1)} copy(bf16[32,4,2,8320]{3,0,2,1:T(8,128)(2,1)S(1)} %get-tuple-element.304) | data formatting | bytes 8519680 | tf_op jit(solution)/shard_map/while/body/eval_jaxpr/convert_element_type | solution.py:40
  109.7 7.7 %convert_element_type.123 = bf16[1,128,16640]{2,1,0:T(8,128)(2,1)} reshape(bf16[32,4,2,8320]{3,2,1,0:T(2,128)(2,1)} %copy.61) | data formatting | bytes 8519680 | tf_op jit(solution)/shard_map/while/body/eval_jaxpr/convert_element_type | solution.py:40
  117.4 4.6 constant_dynamic-update-slice_fusion.2
  122.0 2.0 constant_dynamic-slice_fusion.3
  124.3 17.7 %multiply_add_fusion.2 = (f32[32,4,1,8320]{3,0,2,1:T(8,128)S(1)}, f32[32,4,1,8320]{3,0,2,1:T(8,128)S(1)}) fusion(f32[32,8320]{1,0:T(8,128)S(1)} %get-tuple-element.295, s32[32,4]{0,1:T(4,128)S(1)} %get-tuple-element.296, s32[8320]{0:T(1024)S(1)} %get-tuple-element.297, s32[32,4]{0,1:T(4,128)S(1)} %get-tuple-element.298, ...), kind=kLoop, calls=%fused_computation.13.clone.1 | loop fusion | flops 23429120 | bytes 10717184 | tf_op jit(solution)/shard_map/while/body/eval_jaxpr/add | solution.py:37
  145.0 2.1 mul.436
  148.7 5.3 %copy.61 = bf16[32,4,2,8320]{3,2,1,0:T(2,128)(2,1)} copy(bf16[32,4,2,8320]{3,0,2,1:T(8,128)(2,1)S(1)} %get-tuple-element.304) | data formatting | bytes 8519680 | tf_op jit(solution)/shard_map/while/body/eval_jaxpr/convert_element_type | solution.py:40
  154.0 7.7 %convert_element_type.123 = bf16[1,128,16640]{2,1,0:T(8,128)(2,1)} reshape(bf16[32,4,2,8320]{3,2,1,0:T(2,128)(2,1)} %copy.61) | data formatting | bytes 8519680 | tf_op jit(solution)/shard_map/while/body/eval_jaxpr/convert_element_type | solution.py:40
  161.7 4.6 constant_dynamic-update-slice_fusion.2
  166.3 2.0 constant_dynamic-slice_fusion.3
  168.6 17.7 %multiply_add_fusion.2 = (f32[32,4,1,8320]{3,0,2,1:T(8,128)S(1)}, f32[32,4,1,8320]{3,0,2,1:T(8,128)S(1)}) fusion(f32[32,8320]{1,0:T(8,128)S(1)} %get-tuple-element.295, s32[32,4]{0,1:T(4,128)S(1)} %get-tuple-element.296, s32[8320]{0:T(1024)S(1)} %get-tuple-element.297, s32[32,4]{0,1:T(4,128)S(1)} %get-tuple-element.298, ...), kind=kLoop, calls=%fused_computation.13.clone.1 | loop fusion | flops 23429120 | bytes 10717184 | tf_op jit(solution)/shard_map/while/body/eval_jaxpr/add | solution.py:37
  189.3 2.1 mul.436
  193.0 5.3 %copy.61 = bf16[32,4,2,8320]{3,2,1,0:T(2,128)(2,1)} copy(bf16[32,4,2,8320]{3,0,2,1:T(8,128)(2,1)S(1)} %get-tuple-element.304) | data formatting | bytes 8519680 | tf_op jit(solution)/shard_map/while/body/eval_jaxpr/convert_element_type | solution.py:40
  198.3 7.7 %convert_element_type.123 = bf16[1,128,16640]{2,1,0:T(8,128)(2,1)} reshape(bf16[32,4,2,8320]{3,2,1,0:T(2,128)(2,1)} %copy.61) | data formatting | bytes 8519680 | tf_op jit(solution)/shard_map/while/body/eval_jaxpr/convert_element_type | solution.py:40
  206.0 4.6 constant_dynamic-update-slice_fusion.2
  210.6 2.0 constant_dynamic-slice_fusion.3
  212.9 17.7 %multiply_add_fusion.2 = (f32[32,4,1,8320]{3,0,2,1:T(8,128)S(1)}, f32[32,4,1,8320]{3,0,2,1:T(8,128)S(1)}) fusion(f32[32,8320]{1,0:T(8,128)S(1)} %get-tuple-element.295, s32[32,4]{0,1:T(4,128)S(1)} %get-tuple-element.296, s32[8320]{0:T(1024)S(1)} %get-tuple-element.297, s32[32,4]{0,1:T(4,128)S(1)} %get-tuple-element.298, ...), kind=kLoop, calls=%fused_computation.13.clone.1 | loop fusion | flops 23429120 | bytes 10717184 | tf_op jit(solution)/shard_map/while/body/eval_jaxpr/add | solution.py:37
  233.6 2.1 mul.436
  237.3 5.3 %copy.61 = bf16[32,4,2,8320]{3,2,1,0:T(2,128)(2,1)} copy(bf16[32,4,2,8320]{3,0,2,1:T(8,128)(2,1)S(1)} %get-tuple-element.304) | data formatting | bytes 8519680 | tf_op jit(solution)/shard_map/while/body/eval_jaxpr/convert_element_type | solution.py:40
  242.6 7.7 %convert_element_type.123 = bf16[1,128,16640]{2,1,0:T(8,128)(2,1)} reshape(bf16[32,4,2,8320]{3,2,1,0:T(2,128)(2,1)} %copy.61) | data formatting | bytes 8519680 | tf_op jit(solution)/shard_map/while/body/eval_jaxpr/convert_element_type | solution.py:40
  250.3 4.6 constant_dynamic-update-slice_fusion.2
  255.1 71.1 %pmax.7 = f32[128]{0:T(128)S(1)} all-reduce(f32[128]{0:T(128)S(1)} %reduce_max.12), channel_id=1, replica_groups=mesh['img'=8,'ori'=32] {'ori'}, use_global_device_ids=true, to_apply=%region_4.5 | all-reduce | flops 128 | bytes 1024 | tf_op jit(solution)/shard_map/pmax | solution.py:95
  326.5 69.8 %psum.7 = f32[128]{0:T(128)S(1)} all-reduce(f32[128]{0:T(128)S(1)} %reduce_sum.22), channel_id=1, replica_groups=mesh['img'=8,'ori'=32] {'ori'}, use_global_device_ids=true, to_apply=%region_6.7 | all-reduce | flops 128 | bytes 1024 | tf_op jit(solution)/shard_map/psum | solution.py:96
  396.6 10.3 %convolution_convert_fusion = bf16[64,16640]{1,0:T(8,128)(2,1)} fusion(bf16[512,64]{1,0:T(8,128)(2,1)S(1)} %bitcast.85, bf16[512,16640]{1,0:T(8,128)(2,1)} %bitcast.82), kind=kOutput, calls=%fused_computation.47 | convolution fusion | flops 1091584000 | bytes 19234816 | tf_op jit(solution)/shard_map/dot_general | solution.py:103
  407.6 90.0 %reduce-scatter.2.cloned.1.call-done = bf16[8,16640]{1,0:T(8,128)(2,1)} async-done(((bf16[64,16640]{1,0:T(8,128)(2,1)}), bf16[8,16640]{1,0:T(8,128)(2,1)}) %reduce-scatter.2.cloned.1.call-update) | async-done | bytes 266256 | tf_op jit(solution)/shard_map/reduce_scatter | solution.py:102
  (101 shorter events, 29.3 us)
Async XLA Ops:
  7.2 70.6 %all-gather.2.cloned.1.call-start = ((), (), s32[]{:S(2)}) async-start(), calls=%async_computation.1 | async-start | bytes 4392960 | tf_op jit(solution)/shard_map/all_gather | solution.py:64
  7.9 489.6 %reduce-scatter.2.cloned.1.call-start = ((), (), s32[]{:S(2)}) async-start(), calls=%async_computation.2 | async-start | bytes 2396160 | tf_op jit(solution)/shard_map/reduce_scatter | solution.py:102
  64.8 10.4 %copy-start.2 = (f32[64,8320]{1,0:T(8,128)S(1)}, f32[64,8320]{1,0:T(8,128)}, u32[]{:S(2)}) copy-start(f32[64,8320]{1,0:T(8,128)} %param.10) | copy-start | bytes 6389764
  64.8 10.4 %copy-start.4 = (f32[8320]{0:T(1024)S(1)}, f32[8320]{0:T(1024)}, u32[]{:S(2)}) copy-start(f32[8320]{0:T(1024)} %param.11) | copy-start | bytes 99844
  98.8 1.3 copy-start
  100.7 2.5 copy-start.1
  117.4 4.6 copy-start.3
  143.0 1.3 copy-start
  145.0 2.5 copy-start.1
  161.7 4.6 copy-start.3
  187.4 1.3 copy-start
  189.3 2.5 copy-start.1
  206.0 4.6 copy-start.3
  231.7 1.3 copy-start
  233.6 2.5 copy-start.1
  250.3 4.6 copy-start.3
Sparse Core Ops, SparseCore 0:
  9.9 67.8 all-gather.1
  407.1 90.3 reduce-scatter.1
where the time goes:
time: 508 us; the launch traced here: 506 us
  blocking collectives  195 us (38%)
  local copies, waits for them, and re-layouts  97.1 us (19%)
  waiting for transfers between devices  90.9 us (18%)
  other arithmetic  86 us (17%)
  matrix products  22.2 us (4%)
  between operations  14.8 us (3%)
    reduce_scatter x1, waiting for transfers between devices, per_device(): lax.psum_scatter(lax.dot_general(chosen, flat_prepared, (((0,), (0,)), ((...  90 us
    pmax x1, blocking collectives, per_device(): largest = lax.pmax(local_top, 'ori')  71.1 us
    add x4, other arithmetic, shifted_weighted(): real_part * cosine + imag_part * sine_part  71 us
    psum x1, blocking collectives, per_device(): lax.psum(jnp.sum(jnp.exp(piece_out - largest[:, None, None]), axis=(1, 2)...  69.8 us
    convert_element_type x8, local copies, waits for them, and re-layouts, shifted_weighted(): return (shifted * rows_ctf[:, None, None, :]).astype(jnp.bfloat16)  51.9 us
    all_gather x1, blocking collectives, per_device(): offsets = lax.all_gather(shifts, 'ori', axis=0, tiled=True)  46.9 us
    dynamic_update_slice x4, local copies, waits for them, and re-layouts, per_device(): lax.map(one_block, (block.reshape(count // width, width, 2, pixels), offs...  18.4 us
    dot_general x1, matrix products, per_device(): lax.dot_general(chosen, flat_prepared, (((0,), (0,)), ((), ())), preferre...  10.3 us
  transfers between devices with their start and end apart: 2, of which 2 were waited for; matrix products, arithmetic and copies ran while one was open for 3% of the time, Pallas kernels for 0%

commit v1 on v0

v1 whole, which is shorter than its diff:
```python
import math

import jax
import jax.numpy as jnp
import numpy as np
from jax import lax
from jax.experimental import pallas as pl
from jax.experimental.pallas import tpu as pltpu
from jax.sharding import PartitionSpec as P

KY = 128
KX = 65
LANES = 128
NX, NZ, NY = 4, 4, 4
BLOCKS = NZ * NY
TRANS = 4
TILES = 33
HALF = TILES * LANES
SHIFT = 32 * LANES
HALF_A = 17 * LANES
CHUNKS = 11
CHUNK_TILES = TILES // CHUNKS
CW = CHUNK_TILES * 2 * LANES
OTHERS = [(dz, dy) for dz in range(NZ) for dy in range(NY) if (dz, dy) != (0, 0)]
F32 = jnp.float32
BF16 = jnp.bfloat16
NT = (((1,), (1,)), ((), ()))
HI = lax.Precision.HIGHEST


def kernel(
    img_ref, proj_ref, ctf_ref, noise_ref, trig_ref, shift_ref, class_ref,
    out_ref, ev_ref,
    placed, ometa, pair, pmeta, smeta, gath, praw, ctfh, weights, norms, onehot, ctfrows, vtab, prep,
    score, pscore, stats, post, part, from_a, from_b, from_p, from_m, zsend, zrecv, keep, fin,
    loc_sem, core_s, core_r, meta_s, meta_r, stat_s, stat_r, z_s, z_r,
    yp_s, ym_s, yl_r, yr_r, fa_s, fb_s, fa_r, fb_r, sc_s, sc_r,
    a_s, b_s, a_r, b_r, p_s, m_s, p_r, m_r, w_s, w_r, f_s, f_r,
):
    img = lax.axis_index("img")
    ori = lax.axis_index("ori")
    x, zh = img // 2, img % 2
    core, y, zl = ori % 2, (ori // 2) % 4, ori // 8
    xp, xm, x2 = (x + 1) % 4, (x + 3) % 4, (x + 2) % 4
    yp, ym, y2 = (y + 1) % 4, (y + 3) % 4, (y + 2) % 4
    own = zl * 4 + y

    def dev(x_=x, zh_=zh, zl_=zl, y_=y, core_=core):
        return (x_ * 2 + zh_, (zl_ * 4 + y_) * 2 + core_)

    def send(src, dst, ss, rs, target):
        return pltpu.make_async_remote_copy(
            src_ref=src, dst_ref=dst, send_sem=ss, recv_sem=rs,
            device_id=target, device_id_type=pl.DeviceIdType.MESH,
        )

    peer = dev(core_=1 - core)
    others = [dev(zl_=(zl + dz) % 4, y_=(y + dy) % 4) for dz, dy in OTHERS]
    right, left = dev(x_=xp), dev(x_=xm)
    up, down = dev(y_=yp), dev(y_=ym)
    across = dev(zh_=1 - zh)

    barrier = pltpu.get_barrier_semaphore()
    greeted = [peer, *others, right, left, across]
    for target in greeted:
        pl.semaphore_signal(barrier, inc=1, device_id=target, device_id_type=pl.DeviceIdType.MESH)

    mine = pl.ds(pl.multiple_of(core * SHIFT, LANES), HALF)
    theirs = pl.ds(pl.multiple_of((1 - core) * SHIFT, LANES), HALF)
    ctf_copy = pltpu.make_async_copy(ctf_ref.at[:, mine], ctfh, loc_sem.at[0])
    proj_copy = pltpu.make_async_copy(proj_ref.at[:, mine], praw.at[core], loc_sem.at[1])
    ctf_copy.start()
    proj_copy.start()

    lane = lax.broadcasted_iota(jnp.int32, (8, LANES), 1)
    place = lax.broadcasted_iota(jnp.int32, (8, LANES), 0)
    held_here = (place >= 4) == (core == 1)

    def lay_out(s, carry):
        cols = pl.ds(pl.multiple_of(s * LANES, LANES), LANES)
        straight = img_ref[:, cols].astype(F32)
        swapped = pltpu.roll(straight, 4, 0)
        low = jnp.where(core == 0, straight, swapped)
        high = jnp.where(core == 0, swapped, straight)
        both = jnp.concatenate([low, high], axis=0)
        seen = jnp.concatenate([held_here, held_here], axis=0)
        placed[:, cols] = jnp.where(seen, both, 0.0).astype(BF16)
        return carry

    lax.fori_loop(0, 65, lay_out, 0, unroll=5)
    meta = jnp.zeros((8, LANES), jnp.int32)
    for i in range(4):
        row = place == i + 4 * core
        for t in range(TRANS):
            for k in range(2):
                spot = jnp.logical_and(row, lane == 2 * t + k)
                meta = jnp.where(spot, shift_ref[i, k, t], meta)
        meta = jnp.where(jnp.logical_and(row, lane == 8), class_ref[i], meta)
    meta = meta.astype(F32)
    ometa[...] = jnp.concatenate([meta, jnp.zeros_like(meta)], axis=0).astype(BF16)

    pl.semaphore_wait(barrier, len(greeted))

    pair_copy = send(placed.at[:, theirs], pair, core_s.at[0], core_r.at[0], peer)
    pmeta_copy = send(ometa, pmeta, core_s.at[1], core_r.at[1], peer)
    praw_copy = send(proj_ref.at[:, theirs], praw.at[core], core_s.at[2], core_r.at[2], peer)
    pmeta_copy.start()
    pair_copy.start()
    praw_copy.start()

    pmeta_copy.wait_recv()
    smeta[own] = ometa[...] + pmeta[...]
    meta_copies = [
        send(smeta.at[own], smeta.at[own], meta_s.at[n], meta_r.at[n], target)
        for n, target in enumerate(others)
    ]
    for copy in meta_copies:
        copy.start()

    pair_copy.wait_recv()
    gath[own] = placed[:, mine] + pair[...]

    b0, b1 = zl % 2, zl // 2

    def pick(table):
        low = (1 - b0) * table[0] + b0 * table[1]
        high = (1 - b0) * table[2] + b0 * table[3]
        return (1 - b1) * low + b1 * high

    order = [zl, pick([1, 0, 3, 2]), pick([2, 2, 1, 1]), pick([3, 3, 0, 0])]

    def z_copy(zq, step, target):
        b = zq * 4 + y
        return send(gath.at[b], gath.at[b], z_s.at[step], z_r.at[zq], target)

    z_right = [z_copy(order[q], q, dev(zl_=zl + 1)) for q in range(4)]
    z_left = [z_copy(order[q], 4 + q, dev(zl_=zl - 1)) for q in range(4)]
    goes_right = [zl < 3] + [jnp.logical_and(order[q] < zl, zl < 3) for q in (1, 2, 3)]
    goes_left = [zl > 0] + [jnp.logical_and(order[q] > zl, zl > 0) for q in (1, 2, 3)]
    y_up = [
        send(gath.at[order[q] * 4 + y], gath.at[order[q] * 4 + y], yp_s.at[q], yl_r.at[q], up)
        for q in range(4)
    ]
    y_down = [
        send(gath.at[order[q] * 4 + y], gath.at[order[q] * 4 + y], ym_s.at[q], yr_r.at[q], down)
        for q in range(4)
    ]
    first, second = pl.ds(0, HALF_A), pl.ds(HALF_A, HALF - HALF_A)
    fwd_up, fwd_down = [], []
    for q in range(4):
        low = gath.at[order[q] * 4 + ym, :, first]
        high = gath.at[order[q] * 4 + yp, :, second]
        fwd_up.append(send(low, low, fa_s.at[q], fa_r.at[q], up))
        fwd_down.append(send(high, high, fb_s.at[q], fb_r.at[q], down))

    def launch(q):
        pl.when(goes_right[q])(lambda: z_right[q].start())
        pl.when(goes_left[q])(lambda: z_left[q].start())
        y_up[q].start()
        y_down[q].start()

    launch(0)

    def fill_rows(s, carry):
        p = (s + 32 * core) * LANES + lane
        vtab[s] = lax.shift_right_logical(p * 64528, 22)
        return carry

    lax.fori_loop(0, TILES, fill_rows, 0)

    for copy in meta_copies:
        copy.wait_recv()

    lane2 = lax.broadcasted_iota(jnp.int32, (8, 256), 1)

    def fill_onehot(b, carry):
        classes = smeta[b].astype(F32)[0:8, 8:9].astype(jnp.int32)
        hit = jnp.logical_and(lane2 % 64 == classes, lane2 < 192)
        onehot[pl.ds(pl.multiple_of(b * 8, 8), 8), :] = hit.astype(F32)
        return carry

    lax.fori_loop(0, BLOCKS, fill_onehot, 0)
    ctf_copy.wait()

    def pieces(value):
        one = value.astype(BF16)
        rest = value - one.astype(F32)
        two = rest.astype(BF16)
        three = (rest - two.astype(F32)).astype(BF16)
        return one, two, three

    def fill_ctf(s, carry):
        cols = pl.ds(pl.multiple_of(s * 384, 384), 384)
        one, two, three = pieces(ctfh[:, cols])
        ctfrows[:, cols] = jnp.dot(
            onehot[...].astype(BF16),
            jnp.concatenate([one, two, three, one], axis=0),
            preferred_element_type=F32,
        )
        return carry

    lax.fori_loop(0, TILES // 3, fill_ctf, 0)

    def weigh(s, total):
        cols = pl.ds(pl.multiple_of(s * LANES, LANES), LANES)
        first_ = praw[0, :, cols].astype(F32).reshape(2, 8, 1, 8, LANES)
        second_ = praw[1, :, cols].astype(F32).reshape(2, 8, 1, 8, LANES)
        both = jnp.concatenate([first_, second_], axis=2).reshape(2, 128, LANES)
        counted = 1 - core * (1 - jnp.minimum(s, 1))
        noise = noise_ref[pl.ds(core * 32 + s, 1), :] * counted.astype(F32)
        scaled = (both * noise[None]).astype(BF16)
        weights[:, pl.ds(pl.multiple_of(s * 256, 256), LANES)] = scaled[0]
        weights[:, pl.ds(pl.multiple_of(s * 256 + 128, 128), LANES)] = scaled[1]
        power = both[0] * both[0] + both[1] * both[1]
        ctf = ctfh[:, cols]
        p1, p2, p3 = pieces(power)
        c1, c2, c3 = pieces(ctf * ctf * noise)
        return total + lax.dot_general(
            jnp.concatenate([p1, p2, p3, p1, p2, p1], axis=1),
            jnp.concatenate([c1, c1, c1, c2, c2, c3], axis=1),
            NT, preferred_element_type=F32,
        )

    cosine = trig_ref[0:8, :]
    sine = trig_ref[8:16, :]

    def prepare(b):
        meta = smeta[b].astype(F32)[0:8, :].astype(jnp.int32)
        base, slope = [], []
        for t in range(TRANS):
            sx = meta[:, 2 * t : 2 * t + 1]
            sy = meta[:, 2 * t + 1 : 2 * t + 2]
            base.append(lane * sx)
            slope.append(jnp.broadcast_to(sy - KX * sx, (8, LANES)))

        def body(s, carry):
            cols = pl.ds(pl.multiple_of(s * LANES, LANES), LANES)
            block = gath[b, :, cols].astype(F32)
            ctf = ctfrows[pl.ds(pl.multiple_of(b * 8, 8), 8), cols]
            real, imag = block[0:8] * ctf, block[8:16] * ctf
            height = vtab[s]
            reals, imags = [], []
            for t in range(TRANS):
                index = (base[t] + height * slope[t]) & (KY - 1)
                c = jnp.take_along_axis(cosine, index, axis=1)
                si = jnp.take_along_axis(sine, index, axis=1)
                reals.append(real * c + imag * si)
                imags.append(imag * c - real * si)
            for h in range(2):
                at = pl.ds(pl.multiple_of(b * 32 + h * 16, 16), 16)
                prep[at, pl.ds(pl.multiple_of(s * 256, 256), LANES)] = jnp.concatenate(
                    reals[2 * h : 2 * h + 2], axis=0
                ).astype(BF16)
                prep[at, pl.ds(pl.multiple_of(s * 256 + 128, 128), LANES)] = jnp.concatenate(
                    imags[2 * h : 2 * h + 2], axis=0
                ).astype(BF16)
            return carry

        lax.fori_loop(0, TILES, body, 0, unroll=11)

    def score_group(g):
        rows = pl.ds(pl.multiple_of(g * 128, 128), 128)

        def body(i, total):
            cols = pl.ds(pl.multiple_of(i * 768, 768), 768)
            return total + lax.dot_general(
                weights[:, cols], prep[rows, cols], NT, preferred_element_type=F32
            )

        cross = lax.fori_loop(0, TILES // 3, body, jnp.zeros((128, 128), F32))
        picked = onehot[pl.ds(pl.multiple_of(g * 32, 32), 32), 0:LANES].reshape(4, 1, 8, LANES)
        picked = jnp.concatenate([picked] * TRANS, axis=1).reshape(128, LANES)
        norm = lax.dot_general(
            norms[...], picked[:, :64], NT, precision=HI, preferred_element_type=F32
        )
        score[g] = cross - norm

    sc_copies = [
        send(score.at[order[q]], pscore.at[order[q]], sc_s.at[q], sc_r.at[q], peer)
        for q in range(4)
    ]

    def finish(q):
        fwd_up[q].wait_recv()
        fwd_down[q].wait_recv()
        prepare(order[q] * 4 + y2)
        score_group(order[q])
        sc_copies[q].start()

    def arrive(q):
        z_right[q].wait_recv()
        launch(q)

    def forward(q):
        y_up[q].wait_recv()
        fwd_up[q].start()
        y_down[q].wait_recv()
        fwd_down[q].start()

    def prepare_three(q):
        def three(i, carry):
            prepare(order[q] * 4 + (y + 3 + i) % 4)
            return carry

        lax.fori_loop(0, 3, three, 0)

    arrive(1)
    forward(0)
    prepare_three(0)
    arrive(2)
    forward(1)
    proj_copy.wait()
    praw_copy.wait_recv()
    norms[...] = 0.5 * lax.fori_loop(0, TILES, weigh, jnp.zeros((128, 64), F32), unroll=3)
    arrive(3)
    prepare_three(1)
    forward(2)
    finish(0)
    prepare_three(2)
    forward(3)
    finish(1)
    prepare_three(3)
    finish(2)
    finish(3)

    stats[own] = jnp.zeros((16, LANES), F32)
    for copy in sc_copies:
        copy.wait_recv()
    for g in range(4):
        whole = score[g] + pscore[g]
        pscore[g] = whole
        top = jnp.max(whole, axis=0, keepdims=True)
        stats[own, g : g + 1, :] = top
        stats[own, 8 + g : 9 + g, :] = jnp.sum(jnp.exp(whole - top), axis=0, keepdims=True)
    stat_copies = [
        send(stats.at[own], stats.at[own], stat_s.at[n], stat_r.at[n], target)
        for n, target in enumerate(others)
    ]
    for copy in stat_copies:
        copy.start()
    for copy in stat_copies:
        copy.wait_recv()
    tops = [stats[b, 0:8, :] for b in range(BLOCKS)]
    top = tops[0]
    for b in range(1, BLOCKS):
        top = jnp.maximum(top, tops[b])
    total = jnp.zeros((8, LANES), F32)
    for b in range(BLOCKS):
        total += stats[b, 8:16, :] * jnp.exp(tops[b] - top)
    held = lax.broadcasted_iota(jnp.int32, (8, LANES), 1) % 32

    def turn(value, by):
        inside = pltpu.roll(value, by, 1)
        wrapped = pltpu.roll(value, by + LANES - 32, 1)
        return jnp.where(held >= by, inside, wrapped)

    largest = jnp.maximum(top, turn(top, 8))
    largest = jnp.maximum(largest, turn(largest, 16))
    total = total * jnp.exp(top - largest)
    total = total + turn(total, 8)
    total = total + turn(total, 16)
    evidence = largest + jnp.log(total)
    own_row = jnp.sum(jnp.where(place == zl, evidence, 0.0), axis=0, keepdims=True)
    ev_ref[...] = pltpu.roll(jnp.broadcast_to(own_row, (8, LANES)), 128 - (y * 32 + core * 4), 1)
    for g in range(4):
        post[:, g * 128 : (g + 1) * 128] = (
            jnp.exp(pscore[g] - evidence[g : g + 1, :]) * 2048.0
        ).astype(BF16)

    def copy_a(c):
        return send(part.at[c, 2 * x2], from_a.at[c], a_s.at[c], a_r.at[c], right)

    def copy_b(c):
        return send(part.at[c, 2 * x2 + 1], from_b.at[c], b_s.at[c], b_r.at[c], left)

    def copy_p(c):
        return send(part.at[c, pl.ds(2 * xp, 2)], from_p.at[c], p_s.at[c], p_r.at[c], right)

    def copy_m(c):
        return send(part.at[c, pl.ds(2 * xm, 2)], from_m.at[c], m_s.at[c], m_r.at[c], left)

    def copy_w(c):
        return send(zsend.at[c], zrecv.at[c], w_s.at[c], w_r.at[c], across)

    def copy_f(c):
        other = pl.ds(pl.multiple_of((1 - core) * 8, 8), 8)
        return send(keep.at[c, other], fin.at[c], f_s.at[c], f_r.at[c], peer)

    def write(c, half, value):
        for s in range(CHUNK_TILES):
            at = pl.ds(pl.multiple_of(half * SHIFT + (c * CHUNK_TILES + s) * LANES, LANES), LANES)
            for k in range(2):
                out_ref[k, :, at] = value[:, s * 256 + k * 128 : s * 256 + k * 128 + 128]

    def project(c):
        cols = pl.ds(pl.multiple_of(c * CW, CW), CW)
        sums = jnp.dot(post[...], prep[:, cols], preferred_element_type=F32).astype(BF16)
        for i in range(8):
            part[c, i] = sums[16 * i : 16 * i + 16]
        copy_a(c).start()
        copy_b(c).start()

    def add(into, *others_):
        value = into.astype(F32)
        for other in others_:
            value = value + other.astype(F32)
        return value

    def pass_on(c):
        copy_a(c).wait_recv()
        part[c, 2 * xp] = add(part[c, 2 * xp], from_a[c]).astype(BF16)
        copy_p(c).start()
        copy_b(c).wait_recv()
        part[c, 2 * xm + 1] = add(part[c, 2 * xm + 1], from_b[c]).astype(BF16)
        copy_m(c).start()

    def collect(c):
        copy_p(c).wait_recv()
        copy_m(c).wait_recv()
        far = 1 - zh
        zsend[c] = add(part[c, 2 * x + far], from_p[c, far], from_m[c, far]).astype(BF16)
        copy_w(c).start()
        keep[c] = add(part[c, 2 * x + zh], from_p[c, zh], from_m[c, zh])

    def complete(c):
        copy_w(c).wait_recv()
        keep[c] = keep[c] + zrecv[c].astype(F32)
        copy_f(c).start()
        write(c, core, keep[c, pl.ds(pl.multiple_of(core * 8, 8), 8), :])

    def close(c):
        copy_f(c).wait_recv()
        write(c, 1 - core, fin[c])

    stages = [(0, project), (2, pass_on), (4, collect), (6, complete), (8, close)]

    def step(n, carry):
        for lag, stage in stages:
            here = jnp.logical_and(n >= lag, n < CHUNKS + lag)

            @pl.when(here)
            def _(lag=lag, stage=stage):
                stage(n - lag)

        return carry

    lax.fori_loop(0, CHUNKS + 8, step, 0)

    pmeta_copy.wait_send()
    pair_copy.wait_send()
    praw_copy.wait_send()
    for copy in meta_copies + stat_copies + sc_copies + y_up + y_down + fwd_up + fwd_down:
        copy.wait_send()
    for q in range(4):
        pl.when(goes_right[q])(lambda q=q: z_right[q].wait_send())
        pl.when(goes_left[q])(lambda q=q: z_left[q].wait_send())

    def sent(c, carry):
        for copy in (copy_a, copy_b, copy_p, copy_m, copy_w, copy_f):
            copy(c).wait_send()
        return carry

    lax.fori_loop(0, CHUNKS, sent, 0)


def per_device(images, projections, ctf_table, noise_weight, shifts, defocus):
    local = images.shape[0]
    pixels = images.shape[2]
    rows = images.transpose(1, 0, 2).reshape(2 * local, pixels)
    proj = projections.transpose(1, 0, 2).reshape(128, pixels)
    angles = np.arange(KY) * (2.0 * math.pi / KY)
    trig = np.concatenate([np.tile(np.cos(angles), (8, 1)), np.tile(np.sin(angles), (8, 1))])
    trig = jnp.asarray(trig.astype(np.float32))
    vmem = pl.BlockSpec(memory_space=pltpu.VMEM)
    hbm = pl.BlockSpec(memory_space=pl.ANY)
    smem = pl.BlockSpec(memory_space=pltpu.SMEM)
    dma = pltpu.SemaphoreType.DMA
    sems = [dma((2,)), dma((3,)), dma((3,)), dma((15,)), dma((15,)), dma((15,)), dma((15,))]
    sems += [dma((8,)), dma((4,))] + [dma((4,))] * 10 + [dma((CHUNKS,))] * 12
    sums, evidence = pl.pallas_call(
        kernel,
        out_shape=(
            jax.ShapeDtypeStruct((2, 8, pixels), F32),
            jax.ShapeDtypeStruct((8, LANES), F32),
        ),
        in_specs=[vmem, hbm, hbm, vmem, vmem, smem, smem],
        out_specs=(vmem, vmem),
        scratch_shapes=[
            pltpu.VMEM((16, 65 * LANES), BF16),
            pltpu.VMEM((16, LANES), BF16),
            pltpu.VMEM((16, HALF), BF16),
            pltpu.VMEM((16, LANES), BF16),
            pltpu.VMEM((BLOCKS, 16, LANES), BF16),
            pltpu.VMEM((BLOCKS, 16, HALF), BF16),
            pltpu.VMEM((2, 128, HALF), BF16),
            pltpu.VMEM((64, HALF), F32),
            pltpu.VMEM((128, 2 * HALF), BF16),
            pltpu.VMEM((128, 64), F32),
            pltpu.VMEM((128, 2 * LANES), F32),
            pltpu.VMEM((128, HALF), F32),
            pltpu.VMEM((TILES, 8, LANES), jnp.int32),
            pltpu.VMEM((BLOCKS * 32, 2 * HALF), BF16),
            pltpu.VMEM((4, 128, 128), F32),
            pltpu.VMEM((4, 128, 128), F32),
            pltpu.VMEM((BLOCKS, 16, LANES), F32),
            pltpu.VMEM((128, 512), BF16),
            pltpu.VMEM((CHUNKS, 8, 16, CW), BF16),
            pltpu.VMEM((CHUNKS, 16, CW), BF16),
            pltpu.VMEM((CHUNKS, 16, CW), BF16),
            pltpu.VMEM((CHUNKS, 2, 16, CW), BF16),
            pltpu.VMEM((CHUNKS, 2, 16, CW), BF16),
            pltpu.VMEM((CHUNKS, 16, CW), BF16),
            pltpu.VMEM((CHUNKS, 16, CW), BF16),
            pltpu.VMEM((CHUNKS, 16, CW), F32),
            pltpu.VMEM((CHUNKS, 8, CW), F32),
            *sems,
        ],
        compiler_params=pltpu.CompilerParams(
            collective_id=0, has_side_effects=True, vmem_limit_bytes=56 * 1024 * 1024
        ),
    )(
        rows, proj, ctf_table, noise_weight.reshape(65, LANES), trig,
        shifts.transpose(0, 2, 1), defocus,
    )
    return evidence[0, :local], sums.transpose(1, 0, 2)


def solution(mesh):
    in_specs = (
        P(("img", "ori"), None, None),
        P("ori", None, None),
        P(),
        P(),
        P(("img", "ori"), None, None),
        P(("img", "ori")),
    )
    out_specs = (P(("img", "ori")), P(("ori", "img"), None, None))
    return jax.shard_map(
        per_device, mesh=mesh, in_specs=in_specs, out_specs=out_specs, check_vma=False
    )
```

time: 508 us -> 107 us (0.21)
  blocking collectives: 195 us -> 0 us
  Pallas kernels: 0 us -> 98.3 us
  waiting for transfers between devices: 90.9 us -> 0 us
  local copies, waits for them, and re-layouts: 97.1 us -> 8.1 us
  other arithmetic: 86 us -> 0 us
  matrix products: 22.2 us -> 0 us
  between operations: 14.8 us -> 0.64 us
    pallas_call x0 -> x1, Pallas kernels: none -> 98.3 us  [per_device(): pl.pallas_call(kernel, out_shape=(jax.ShapeDtypeStruct((2, 8, pixels), F3...]
    reduce_scatter x1 -> x0, waiting for transfers between devices: 90 us -> none  [per_device(): lax.psum_scatter(lax.dot_general(chosen, flat_prepared, (((0,), (0,)), ((...]
    pmax x1 -> x0, blocking collectives: 71.1 us -> none  [per_device(): largest = lax.pmax(local_top, 'ori')]
    add x5 -> x0, other arithmetic: 71 us -> none  [the longest x4 71 us: shifted_weighted(): real_part * cosine + imag_part * sine_part]
    psum x1 -> x0, blocking collectives: 69.8 us -> none  [per_device(): lax.psum(jnp.sum(jnp.exp(piece_out - largest[:, None, None]), axis=(1, 2)...]
    convert_element_type x9 -> x0, local copies, waits for them, and re-layouts: 52 us -> none  [the longest x8 51.9 us: shifted_weighted(): return (shifted * rows_ctf[:, None, None, :]).astype(jnp.bfloat16)]
    all_gather x1 -> x0, blocking collectives: 46.9 us -> none  [per_device(): offsets = lax.all_gather(shifts, 'ori', axis=0, tiled=True)]
    dot_general x14 -> x0, matrix products: 22.2 us -> none  [the longest x1 10.3 us: per_device(): lax.dot_general(chosen, flat_prepared, (((0,), (0,)), ((), ())), preferre...]
  transfers between devices with their start and end apart: 2 -> 0, of which waited for: 2 -> 0; matrix products, arithmetic and copies ran while one was open for 3% -> 0% of each run, Pallas kernels for 0% -> 0%
where the time goes in v1:
time: 107 us
  Pallas kernels  98.3 us (92%)
  local copies, waits for them, and re-layouts  8.1 us (8%)
    pallas_call x1, Pallas kernels, per_device(): pl.pallas_call(kernel, out_shape=(jax.ShapeDtypeStruct((2, 8, pixels), F3...  98.3 us
    transpose x1, local copies, waits for them, and re-layouts, per_device(): proj = projections.transpose(1, 0, 2).reshape(128, pixels)  3.15 us

profile of v1, /device:TPU:1, one launch (start us, length us, event | category | flops | bytes accessed | tf_op | source)
XLA Modules:
  0.0 107.1 jit_solution(6526663245561981857)
XLA Ops:
  0.6 1.0 copy.9
  1.6 0.7 reshape.13.img_ref
  2.3 3.2 %copy.10 = bf16[2,64,8320]{2,1,0:T(8,128)(2,1)} copy(bf16[2,64,8320]{2,0,1:T(2,128)(2,1)} %bitcast.9) | data formatting | bytes 4259840 | tf_op jit(solution)/shard_map/transpose | solution.py:470
  5.4 98.3 %shard_map.86 = (f32[2,8,8320]{2,1,0:T(8,128)}, f32[8,128]{1,0:T(8,128)}) custom-call(bf16[8,8320]{1,0:T(8,128)(2,1)} %reshape.13.img_ref, bf16[128,8320]{1,0:T(8,128)(2,1)} %bitcast.8, f32[64,8320]{1,0:T(8,128)} %ctf_ref.1, f32[65,128]{1,0:T(8,128)} %bitcast.12, f32[16,128]{1,0:T(8,128)} %constant.2.clone.trig_ref, s32[4,2,4]{2,1,0:T(2,128)} %bitcast.13, ...), custom_call_target="tpu_custom_call" | custom-call | tf_op jit(solution)/shard_map/pallas_call | solution.py:480
  103.8 1.2 %slice_bitcast_fusion = f32[4]{0:T(128)} fusion(f32[8,128]{1,0:T(8,128)} %get-tuple-element.4), kind=kLoop, calls=%fused_computation | loop fusion | bytes 32 | tf_op jit(solution)/shard_map/squeeze | solution.py:525
  105.0 2.1 %copy.11 = f32[8,2,8320]{2,1,0:T(2,128)} copy(f32[8,2,8320]{2,0,1:T(8,128)} %bitcast.10) | data formatting | bytes 1064960

commit v2 on v1

--- a/solution.py
+++ b/solution.py
@@ -24,7 +24,6 @@
 OTHERS = [(dz, dy) for dz in range(NZ) for dy in range(NY) if (dz, dy) != (0, 0)]
 F32 = jnp.float32
 BF16 = jnp.bfloat16
-NT = (((1,), (1,)), ((), ()))
 HI = lax.Precision.HIGHEST
 
 
@@ -58,10 +57,10 @@
     others = [dev(zl_=(zl + dz) % 4, y_=(y + dy) % 4) for dz, dy in OTHERS]
     right, left = dev(x_=xp), dev(x_=xm)
     up, down = dev(y_=yp), dev(y_=ym)
-    across = dev(zh_=1 - zh)
+    across = [dev(zh_=1 - zh, core_=k) for k in range(2)]
 
     barrier = pltpu.get_barrier_semaphore()
-    greeted = [peer, *others, right, left, across]
+    greeted = [peer, *others, right, left, *across]
     for target in greeted:
         pl.semaphore_signal(barrier, inc=1, device_id=target, device_id_type=pl.DeviceIdType.MESH)
 
@@ -163,10 +162,12 @@
 
     def fill_rows(s, carry):
         p = (s + 32 * core) * LANES + lane
-        vtab[s] = lax.shift_right_logical(p * 64528, 22)
+        after = lax.shift_right_logical((p + LANES) * 64528, 22)
+        vtab[s] = after - lax.shift_right_logical(p * 64528, 22)
         return carry
 
     lax.fori_loop(0, TILES, fill_rows, 0)
+    top_row = lax.shift_right_logical((32 * core * LANES + lane) * 64528, 22)
 
     for copy in meta_copies:
         copy.wait_recv()
@@ -209,16 +210,16 @@
         counted = 1 - core * (1 - jnp.minimum(s, 1))
         noise = noise_ref[pl.ds(core * 32 + s, 1), :] * counted.astype(F32)
         scaled = (both * noise[None]).astype(BF16)
-        weights[:, pl.ds(pl.multiple_of(s * 256, 256), LANES)] = scaled[0]
-        weights[:, pl.ds(pl.multiple_of(s * 256 + 128, 128), LANES)] = scaled[1]
-        power = both[0] * both[0] + both[1] * both[1]
+        weights[pl.ds(pl.multiple_of(s * 256, 256), LANES), :] = scaled[0].T
+        weights[pl.ds(pl.multiple_of(s * 256 + 128, 128), LANES), :] = scaled[1].T
+        power = (both[0] * both[0] + both[1] * both[1]).T
         ctf = ctfh[:, cols]
         p1, p2, p3 = pieces(power)
         c1, c2, c3 = pieces(ctf * ctf * noise)
-        return total + lax.dot_general(
-            jnp.concatenate([p1, p2, p3, p1, p2, p1], axis=1),
+        return total + jnp.dot(
             jnp.concatenate([c1, c1, c1, c2, c2, c3], axis=1),
-            NT, preferred_element_type=F32,
+            jnp.concatenate([p1, p2, p3, p1, p2, p1], axis=0),
+            preferred_element_type=F32,
         )
 
     cosine = trig_ref[0:8, :]
@@ -226,26 +227,37 @@
 
     def prepare(b):
         meta = smeta[b].astype(F32)[0:8, :].astype(jnp.int32)
-        base, slope = [], []
+
+        def wave(steps):
+            index = steps & (KY - 1)
+            return (
+                jnp.take_along_axis(cosine, index, axis=1),
+                jnp.take_along_axis(sine, index, axis=1),
+            )
+
+        begin, one_row, two_rows = [], [], []
         for t in range(TRANS):
             sx = meta[:, 2 * t : 2 * t + 1]
             sy = meta[:, 2 * t + 1 : 2 * t + 2]
-            base.append(lane * sx)
-            slope.append(jnp.broadcast_to(sy - KX * sx, (8, LANES)))
-
-        def body(s, carry):
+            slope = jnp.broadcast_to(sy - KX * sx, (8, LANES))
+            begin.append(wave(lane * sx + top_row * slope))
+            one_row.append(wave(slope))
+            two_rows.append(wave(2 * slope))
+
+        def body(s, phases):
             cols = pl.ds(pl.multiple_of(s * LANES, LANES), LANES)
             block = gath[b, :, cols].astype(F32)
             ctf = ctfrows[pl.ds(pl.multiple_of(b * 8, 8), 8), cols]
             real, imag = block[0:8] * ctf, block[8:16] * ctf
-            height = vtab[s]
-            reals, imags = [], []
+            single = vtab[s] == 1
+            reals, imags, later = [], [], []
             for t in range(TRANS):
-                index = (base[t] + height * slope[t]) & (KY - 1)
-                c = jnp.take_along_axis(cosine, index, axis=1)
-                si = jnp.take_along_axis(sine, index, axis=1)
+                c, si = phases[t]
                 reals.append(real * c + imag * si)
                 imags.append(imag * c - real * si)
+                mc = jnp.where(single, one_row[t][0], two_rows[t][0])
+                ms = jnp.where(single, one_row[t][1], two_rows[t][1])
+                later.append((c * mc - si * ms, si * mc + c * ms))
             for h in range(2):
                 at = pl.ds(pl.multiple_of(b * 32 + h * 16, 16), 16)
                 prep[at, pl.ds(pl.multiple_of(s * 256, 256), LANES)] = jnp.concatenate(
@@ -254,25 +266,23 @@
                 prep[at, pl.ds(pl.multiple_of(s * 256 + 128, 128), LANES)] = jnp.concatenate(
                     imags[2 * h : 2 * h + 2], axis=0
                 ).astype(BF16)
-            return carry
-
-        lax.fori_loop(0, TILES, body, 0, unroll=11)
+            return tuple(later)
+
+        lax.fori_loop(0, TILES, body, tuple(begin), unroll=11)
 
     def score_group(g):
         rows = pl.ds(pl.multiple_of(g * 128, 128), 128)
 
         def body(i, total):
             cols = pl.ds(pl.multiple_of(i * 768, 768), 768)
-            return total + lax.dot_general(
-                weights[:, cols], prep[rows, cols], NT, preferred_element_type=F32
+            return total + jnp.dot(
+                prep[rows, cols], weights[cols, :], preferred_element_type=F32
             )
 
         cross = lax.fori_loop(0, TILES // 3, body, jnp.zeros((128, 128), F32))
         picked = onehot[pl.ds(pl.multiple_of(g * 32, 32), 32), 0:LANES].reshape(4, 1, 8, LANES)
         picked = jnp.concatenate([picked] * TRANS, axis=1).reshape(128, LANES)
-        norm = lax.dot_general(
-            norms[...], picked[:, :64], NT, precision=HI, preferred_element_type=F32
-        )
+        norm = jnp.dot(picked[:, :64], norms[...], precision=HI, preferred_element_type=F32)
         score[g] = cross - norm
 
     sc_copies = [
@@ -311,7 +321,7 @@
     forward(1)
     proj_copy.wait()
     praw_copy.wait_recv()
-    norms[...] = 0.5 * lax.fori_loop(0, TILES, weigh, jnp.zeros((128, 64), F32), unroll=3)
+    norms[...] = 0.5 * lax.fori_loop(0, TILES, weigh, jnp.zeros((64, 128), F32), unroll=3)
     arrive(3)
     prepare_three(1)
     forward(2)
@@ -327,7 +337,7 @@
     for copy in sc_copies:
         copy.wait_recv()
     for g in range(4):
-        whole = score[g] + pscore[g]
+        whole = (score[g] + pscore[g]).T
         pscore[g] = whole
         top = jnp.max(whole, axis=0, keepdims=True)
         stats[own, g : g + 1, :] = top
@@ -379,8 +389,11 @@
     def copy_m(c):
         return send(part.at[c, pl.ds(2 * xm, 2)], from_m.at[c], m_s.at[c], m_r.at[c], left)
 
-    def copy_w(c):
-        return send(zsend.at[c], zrecv.at[c], w_s.at[c], w_r.at[c], across)
+    def copy_w(c, k):
+        return send(zsend.at[c, k], zrecv.at[c, core], w_s.at[c, k], w_r.at[c, core], across[k])
+
+    def arrived_w(c, half):
+        return send(zsend.at[c, 0], zrecv.at[c, half], w_s.at[c, 0], w_r.at[c, half], across[0])
 
     def copy_f(c):
         other = pl.ds(pl.multiple_of((1 - core) * 8, 8), 8)
@@ -418,21 +431,24 @@
         copy_p(c).wait_recv()
         copy_m(c).wait_recv()
         far = 1 - zh
-        zsend[c] = add(part[c, 2 * x + far], from_p[c, far], from_m[c, far]).astype(BF16)
-        copy_w(c).start()
+        away = add(part[c, 2 * x + far], from_p[c, far], from_m[c, far])
+        for k in range(2):
+            rows = away[8 * k : 8 * k + 8]
+            zsend[c, k] = jnp.concatenate([rows[:, : CW // 2], rows[:, CW // 2 :]], axis=0).astype(BF16)
+            copy_w(c, k).start()
         keep[c] = add(part[c, 2 * x + zh], from_p[c, zh], from_m[c, zh])
+        copy_f(c).start()
 
     def complete(c):
-        copy_w(c).wait_recv()
-        keep[c] = keep[c] + zrecv[c].astype(F32)
-        copy_f(c).start()
-        write(c, core, keep[c, pl.ds(pl.multiple_of(core * 8, 8), 8), :])
-
-    def close(c):
+        for half in range(2):
+            arrived_w(c, half).wait_recv()
         copy_f(c).wait_recv()
-        write(c, 1 - core, fin[c])
-
-    stages = [(0, project), (2, pass_on), (4, collect), (6, complete), (8, close)]
+        here = keep[c, pl.ds(pl.multiple_of(core * 8, 8), 8), :]
+        for half, near in ((core, here), (1 - core, fin[c])):
+            rows = zrecv[c, half].astype(F32)
+            write(c, half, near + jnp.concatenate([rows[0:8], rows[8:16]], axis=1))
+
+    stages = [(0, project), (3, pass_on), (6, collect), (10, complete)]
 
     def step(n, carry):
         for lag, stage in stages:
@@ -444,7 +460,7 @@
 
         return carry
 
-    lax.fori_loop(0, CHUNKS + 8, step, 0)
+    lax.fori_loop(0, CHUNKS + 10, step, 0)
 
     pmeta_copy.wait_send()
     pair_copy.wait_send()
@@ -456,8 +472,10 @@
         pl.when(goes_left[q])(lambda q=q: z_left[q].wait_send())
 
     def sent(c, carry):
-        for copy in (copy_a, copy_b, copy_p, copy_m, copy_w, copy_f):
+        for copy in (copy_a, copy_b, copy_p, copy_m, copy_f):
             copy(c).wait_send()
+        for k in range(2):
+            copy_w(c, k).wait_send()
         return carry
 
     lax.fori_loop(0, CHUNKS, sent, 0)
@@ -476,7 +494,7 @@
     smem = pl.BlockSpec(memory_space=pltpu.SMEM)
     dma = pltpu.SemaphoreType.DMA
     sems = [dma((2,)), dma((3,)), dma((3,)), dma((15,)), dma((15,)), dma((15,)), dma((15,))]
-    sems += [dma((8,)), dma((4,))] + [dma((4,))] * 10 + [dma((CHUNKS,))] * 12
+    sems += [dma((8,)), dma((4,))] + [dma((4,))] * 10 + [dma((CHUNKS,))] * 8 + [dma((CHUNKS, 2))] * 2 + [dma((CHUNKS,))] * 2
     sums, evidence = pl.pallas_call(
         kernel,
         out_shape=(
@@ -494,8 +512,8 @@
             pltpu.VMEM((BLOCKS, 16, HALF), BF16),
             pltpu.VMEM((2, 128, HALF), BF16),
             pltpu.VMEM((64, HALF), F32),
-            pltpu.VMEM((128, 2 * HALF), BF16),
-            pltpu.VMEM((128, 64), F32),
+            pltpu.VMEM((2 * HALF, 128), BF16),
+            pltpu.VMEM((64, 128), F32),
             pltpu.VMEM((128, 2 * LANES), F32),
             pltpu.VMEM((128, HALF), F32),
             pltpu.VMEM((TILES, 8, LANES), jnp.int32),
@@ -509,8 +527,8 @@
             pltpu.VMEM((CHUNKS, 16, CW), BF16),
             pltpu.VMEM((CHUNKS, 2, 16, CW), BF16),
             pltpu.VMEM((CHUNKS, 2, 16, CW), BF16),
-            pltpu.VMEM((CHUNKS, 16, CW), BF16),
-            pltpu.VMEM((CHUNKS, 16, CW), BF16),
+            pltpu.VMEM((CHUNKS, 2, 16, CW // 2), BF16),
+            pltpu.VMEM((CHUNKS, 2, 16, CW // 2), BF16),
             pltpu.VMEM((CHUNKS, 16, CW), F32),
             pltpu.VMEM((CHUNKS, 8, CW), F32),
             *sems,

time: 107 us -> 95.6 us (0.89)
  Pallas kernels: 98.3 us -> 86.7 us
    pallas_call x1, Pallas kernels: 98.3 us -> 86.7 us  [per_device(): pl.pallas_call(kernel, out_shape=(jax.ShapeDtypeStruct((2, 8, pixels), F3...]
where the time goes in v2:
time: 95.6 us; the launch traced here: 95.4 us
  Pallas kernels  86.7 us (91%)
  local copies, waits for them, and re-layouts  8.1 us (8%)
    pallas_call x1, Pallas kernels, per_device(): pl.pallas_call(kernel, out_shape=(jax.ShapeDtypeStruct((2, 8, pixels), F3...  86.7 us
    transpose x1, local copies, waits for them, and re-layouts, per_device(): proj = projections.transpose(1, 0, 2).reshape(128, pixels)  3.15 us
    unnamed x1, local copies, waits for them, and re-layouts  2.11 us

profile of v2, /device:TPU:1, one launch (start us, length us, event | category | flops | bytes accessed | tf_op | source)
XLA Modules:
  0.0 95.4 jit_solution(18284698847390898535)
XLA Ops:
  0.6 1.0 %copy.9 = bf16[2,4,8320]{2,1,0:T(4,128)(2,1)S(1)} copy(bf16[2,4,8320]{2,0,1:T(2,128)(2,1)} %bitcast.11) | data formatting | bytes 266240 | tf_op jit(solution)/shard_map/transpose | solution.py:487
  1.6 0.7 reshape.13.img_ref
  2.3 3.2 %copy.10 = bf16[2,64,8320]{2,1,0:T(8,128)(2,1)} copy(bf16[2,64,8320]{2,0,1:T(2,128)(2,1)} %bitcast.9) | data formatting | bytes 4259840 | tf_op jit(solution)/shard_map/transpose | solution.py:488
  5.4 86.7 %shard_map.86 = (f32[2,8,8320]{2,1,0:T(8,128)}, f32[8,128]{1,0:T(8,128)}) custom-call(bf16[8,8320]{1,0:T(8,128)(2,1)} %reshape.13.img_ref, bf16[128,8320]{1,0:T(8,128)(2,1)} %bitcast.8, f32[64,8320]{1,0:T(8,128)} %ctf_ref.1, f32[65,128]{1,0:T(8,128)} %bitcast.12, f32[16,128]{1,0:T(8,128)} %constant.2.clone.trig_ref, s32[4,2,4]{2,1,0:T(2,128)} %bitcast.13, ...), custom_call_target="tpu_custom_call" | custom-call | tf_op jit(solution)/shard_map/pallas_call | solution.py:498
  92.1 1.2 %slice_bitcast_fusion = f32[4]{0:T(128)} fusion(f32[8,128]{1,0:T(8,128)} %get-tuple-element.4), kind=kLoop, calls=%fused_computation | loop fusion | bytes 32 | tf_op jit(solution)/shard_map/squeeze | solution.py:543
  93.3 2.1 %copy.11 = f32[8,2,8320]{2,1,0:T(2,128)} copy(f32[8,2,8320]{2,0,1:T(8,128)} %bitcast.10) | data formatting | bytes 1064960

commit v3 on v2

--- a/solution.py
+++ b/solution.py
@@ -279,7 +279,7 @@
                 prep[rows, cols], weights[cols, :], preferred_element_type=F32
             )
 
-        cross = lax.fori_loop(0, TILES // 3, body, jnp.zeros((128, 128), F32))
+        cross = lax.fori_loop(0, TILES // 3, body, jnp.zeros((128, 128), F32), unroll=11)
         picked = onehot[pl.ds(pl.multiple_of(g * 32, 32), 32), 0:LANES].reshape(4, 1, 8, LANES)
         picked = jnp.concatenate([picked] * TRANS, axis=1).reshape(128, LANES)
         norm = jnp.dot(picked[:, :64], norms[...], precision=HI, preferred_element_type=F32)
@@ -289,6 +289,17 @@
         send(score.at[order[q]], pscore.at[order[q]], sc_s.at[q], sc_r.at[q], peer)
         for q in range(4)
     ]
+
+    stats[own] = jnp.zeros((16, LANES), F32)
+
+    def summarise(q):
+        sc_copies[q].wait_recv()
+        g = order[q]
+        whole = (score[g] + pscore[g]).T
+        pscore[g] = whole
+        top = jnp.max(whole, axis=0, keepdims=True)
+        stats[own, pl.ds(g, 1), :] = top
+        stats[own, pl.ds(8 + g, 1), :] = jnp.sum(jnp.exp(whole - top), axis=0, keepdims=True)
 
     def finish(q):
         fwd_up[q].wait_recv()
@@ -329,19 +340,14 @@
     prepare_three(2)
     forward(3)
     finish(1)
+    summarise(0)
     prepare_three(3)
     finish(2)
+    summarise(1)
     finish(3)
-
-    stats[own] = jnp.zeros((16, LANES), F32)
-    for copy in sc_copies:
-        copy.wait_recv()
-    for g in range(4):
-        whole = (score[g] + pscore[g]).T
-        pscore[g] = whole
-        top = jnp.max(whole, axis=0, keepdims=True)
-        stats[own, g : g + 1, :] = top
-        stats[own, 8 + g : 9 + g, :] = jnp.sum(jnp.exp(whole - top), axis=0, keepdims=True)
+    summarise(2)
+    summarise(3)
+
     stat_copies = [
         send(stats.at[own], stats.at[own], stat_s.at[n], stat_r.at[n], target)
         for n, target in enumerate(others)

time: 95.6 us -> 89.7 us (0.938)
  Pallas kernels: 86.7 us -> 80.7 us
    pallas_call x1, Pallas kernels: 86.7 us -> 80.7 us  [per_device(): pl.pallas_call(kernel, out_shape=(jax.ShapeDtypeStruct((2, 8, pixels), F3...]
where the time goes in v3:
time: 89.7 us; the launch traced here: 89.5 us
  Pallas kernels  80.7 us (90%)
  local copies, waits for them, and re-layouts  8.1 us (9%)
    pallas_call x1, Pallas kernels, per_device(): pl.pallas_call(kernel, out_shape=(jax.ShapeDtypeStruct((2, 8, pixels), F3...  80.7 us
    transpose x1, local copies, waits for them, and re-layouts, per_device(): proj = projections.transpose(1, 0, 2).reshape(128, pixels)  3.15 us
    unnamed x1, local copies, waits for them, and re-layouts  2.11 us

profile of v3, /device:TPU:1, one launch (start us, length us, event | category | flops | bytes accessed | tf_op | source)
XLA Modules:
  0.0 89.5 jit_solution(14771095531565124481)
XLA Ops:
  0.6 1.0 %copy.9 = bf16[2,4,8320]{2,1,0:T(4,128)(2,1)S(1)} copy(bf16[2,4,8320]{2,0,1:T(2,128)(2,1)} %bitcast.11) | data formatting | bytes 266240 | tf_op jit(solution)/shard_map/transpose | solution.py:493
  1.6 0.7 reshape.13.img_ref
  2.3 3.2 %copy.10 = bf16[2,64,8320]{2,1,0:T(8,128)(2,1)} copy(bf16[2,64,8320]{2,0,1:T(2,128)(2,1)} %bitcast.9) | data formatting | bytes 4259840 | tf_op jit(solution)/shard_map/transpose | solution.py:494
  5.4 80.7 %shard_map.86 = (f32[2,8,8320]{2,1,0:T(8,128)}, f32[8,128]{1,0:T(8,128)}) custom-call(bf16[8,8320]{1,0:T(8,128)(2,1)} %reshape.13.img_ref, bf16[128,8320]{1,0:T(8,128)(2,1)} %bitcast.8, f32[64,8320]{1,0:T(8,128)} %ctf_ref.1, f32[65,128]{1,0:T(8,128)} %bitcast.12, f32[16,128]{1,0:T(8,128)} %constant.2.clone.trig_ref, s32[4,2,4]{2,1,0:T(2,128)} %bitcast.13, ...), custom_call_target="tpu_custom_call" | custom-call | tf_op jit(solution)/shard_map/pallas_call | solution.py:504
  86.2 1.2 %slice_bitcast_fusion = f32[4]{0:T(128)} fusion(f32[8,128]{1,0:T(8,128)} %get-tuple-element.4), kind=kLoop, calls=%fused_computation | loop fusion | bytes 32 | tf_op jit(solution)/shard_map/squeeze | solution.py:549
  87.3 2.1 %copy.11 = f32[8,2,8320]{2,1,0:T(2,128)} copy(f32[8,2,8320]{2,0,1:T(8,128)} %bitcast.10) | data formatting | bytes 1064960

commit v4 on v3

--- a/solution.py
+++ b/solution.py
@@ -31,10 +31,10 @@
     img_ref, proj_ref, ctf_ref, noise_ref, trig_ref, shift_ref, class_ref,
     out_ref, ev_ref,
     placed, ometa, pair, pmeta, smeta, gath, praw, ctfh, weights, norms, onehot, ctfrows, vtab, prep,
-    score, pscore, stats, post, part, from_a, from_b, from_p, from_m, zsend, zrecv, keep, fin,
+    score, pscore, stats, post, part, from_a, from_b, from_p, from_m, zsend, zmid, zrecv, keep, fin,
     loc_sem, core_s, core_r, meta_s, meta_r, stat_s, stat_r, z_s, z_r,
     yp_s, ym_s, yl_r, yr_r, fa_s, fb_s, fa_r, fb_r, sc_s, sc_r,
-    a_s, b_s, a_r, b_r, p_s, m_s, p_r, m_r, w_s, w_r, f_s, f_r,
+    a_s, b_s, a_r, b_r, p_s, m_s, p_r, m_r, v_s, v_r, w_s, w_r, f_s, f_r,
 ):
     img = lax.axis_index("img")
     ori = lax.axis_index("ori")
@@ -57,10 +57,16 @@
     others = [dev(zl_=(zl + dz) % 4, y_=(y + dy) % 4) for dz, dy in OTHERS]
     right, left = dev(x_=xp), dev(x_=xm)
     up, down = dev(y_=yp), dev(y_=ym)
-    across = [dev(zh_=1 - zh, core_=k) for k in range(2)]
+    z = zh * 4 + zl
+
+    def along(steps, core_=core):
+        there = (z + steps) % 8
+        return dev(zh_=there // 4, zl_=there % 4, core_=core_)
+
 
     barrier = pltpu.get_barrier_semaphore()
-    greeted = [peer, *others, right, left, *across]
+    greeted = [peer, *others, right, left]
+    greeted += [along(steps, k) for steps in (2, 6) for k in range(2)]
     for target in greeted:
         pl.semaphore_signal(barrier, inc=1, device_id=target, device_id_type=pl.DeviceIdType.MESH)
 
@@ -395,11 +401,17 @@
     def copy_m(c):
         return send(part.at[c, pl.ds(2 * xm, 2)], from_m.at[c], m_s.at[c], m_r.at[c], left)
 
+    def copy_v(c):
+        return send(zsend.at[c], zmid.at[c], v_s.at[c], v_r.at[c], along(2 + 4 * (c % 2)))
+
     def copy_w(c, k):
-        return send(zsend.at[c, k], zrecv.at[c, core], w_s.at[c, k], w_r.at[c, core], across[k])
+        return send(
+            zmid.at[c, k], zrecv.at[c, core], w_s.at[c, k], w_r.at[c, core],
+            along(2 + 4 * (c % 2), k),
+        )
 
     def arrived_w(c, half):
-        return send(zsend.at[c, 0], zrecv.at[c, half], w_s.at[c, 0], w_r.at[c, half], across[0])
+        return send(zmid.at[c, 0], zrecv.at[c, half], w_s.at[c, 0], w_r.at[c, half], along(2))
 
     def copy_f(c):
         other = pl.ds(pl.multiple_of((1 - core) * 8, 8), 8)
@@ -441,9 +453,14 @@
         for k in range(2):
             rows = away[8 * k : 8 * k + 8]
             zsend[c, k] = jnp.concatenate([rows[:, : CW // 2], rows[:, CW // 2 :]], axis=0).astype(BF16)
-            copy_w(c, k).start()
+        copy_v(c).start()
         keep[c] = add(part[c, 2 * x + zh], from_p[c, zh], from_m[c, zh])
         copy_f(c).start()
+
+    def relay(c):
+        copy_v(c).wait_recv()
+        for k in range(2):
+            copy_w(c, k).start()
 
     def complete(c):
         for half in range(2):
@@ -454,7 +471,7 @@
             rows = zrecv[c, half].astype(F32)
             write(c, half, near + jnp.concatenate([rows[0:8], rows[8:16]], axis=1))
 
-    stages = [(0, project), (3, pass_on), (6, collect), (10, complete)]
+    stages = [(0, project), (3, pass_on), (6, collect), (8, relay), (11, complete)]
 
     def step(n, carry):
         for lag, stage in stages:
@@ -466,7 +483,7 @@
 
         return carry
 
-    lax.fori_loop(0, CHUNKS + 10, step, 0)
+    lax.fori_loop(0, CHUNKS + 11, step, 0)
 
     pmeta_copy.wait_send()
     pair_copy.wait_send()
@@ -478,7 +495,7 @@
         pl.when(goes_left[q])(lambda q=q: z_left[q].wait_send())
 
     def sent(c, carry):
-        for copy in (copy_a, copy_b, copy_p, copy_m, copy_f):
+        for copy in (copy_a, copy_b, copy_p, copy_m, copy_v, copy_f):
             copy(c).wait_send()
         for k in range(2):
             copy_w(c, k).wait_send()
@@ -500,7 +517,7 @@
     smem = pl.BlockSpec(memory_space=pltpu.SMEM)
     dma = pltpu.SemaphoreType.DMA
     sems = [dma((2,)), dma((3,)), dma((3,)), dma((15,)), dma((15,)), dma((15,)), dma((15,))]
-    sems += [dma((8,)), dma((4,))] + [dma((4,))] * 10 + [dma((CHUNKS,))] * 8 + [dma((CHUNKS, 2))] * 2 + [dma((CHUNKS,))] * 2
+    sems += [dma((8,)), dma((4,))] + [dma((4,))] * 10 + [dma((CHUNKS,))] * 10 + [dma((CHUNKS, 2))] * 2 + [dma((CHUNKS,))] * 2
     sums, evidence = pl.pallas_call(
         kernel,
         out_shape=(
@@ -535,6 +552,7 @@
             pltpu.VMEM((CHUNKS, 2, 16, CW), BF16),
             pltpu.VMEM((CHUNKS, 2, 16, CW // 2), BF16),
             pltpu.VMEM((CHUNKS, 2, 16, CW // 2), BF16),
+            pltpu.VMEM((CHUNKS, 2, 16, CW // 2), BF16),
             pltpu.VMEM((CHUNKS, 16, CW), F32),
             pltpu.VMEM((CHUNKS, 8, CW), F32),
             *sems,

time: 89.7 us -> 93.7 us (1.045)
  Pallas kernels: 80.7 us -> 84.6 us
    pallas_call x1, Pallas kernels: 80.7 us -> 84.6 us  [per_device(): pl.pallas_call(kernel, out_shape=(jax.ShapeDtypeStruct((2, 8, pixels), F3...]
where the time goes in v4:
time: 93.7 us; the launch traced here: 93.4 us
  Pallas kernels  84.6 us (90%)
  local copies, waits for them, and re-layouts  8.1 us (9%)
    pallas_call x1, Pallas kernels, per_device(): pl.pallas_call(kernel, out_shape=(jax.ShapeDtypeStruct((2, 8, pixels), F3...  84.6 us
    transpose x1, local copies, waits for them, and re-layouts, per_device(): proj = projections.transpose(1, 0, 2).reshape(128, pixels)  3.15 us
    unnamed x1, local copies, waits for them, and re-layouts  2.11 us

profile of v4, /device:TPU:1, one launch (start us, length us, event | category | flops | bytes accessed | tf_op | source)
XLA Modules:
  0.0 93.4 jit_solution(14527665457309271825)
XLA Ops:
  0.6 1.0 %copy.9 = bf16[2,4,8320]{2,1,0:T(4,128)(2,1)S(1)} copy(bf16[2,4,8320]{2,0,1:T(2,128)(2,1)} %bitcast.11) | data formatting | bytes 266240 | tf_op jit(solution)/shard_map/transpose | solution.py:510
  1.6 0.7 reshape.13.img_ref
  2.3 3.2 %copy.10 = bf16[2,64,8320]{2,1,0:T(8,128)(2,1)} copy(bf16[2,64,8320]{2,0,1:T(2,128)(2,1)} %bitcast.9) | data formatting | bytes 4259840 | tf_op jit(solution)/shard_map/transpose | solution.py:511
  5.4 84.6 %shard_map.86 = (f32[2,8,8320]{2,1,0:T(8,128)}, f32[8,128]{1,0:T(8,128)}) custom-call(bf16[8,8320]{1,0:T(8,128)(2,1)} %reshape.13.img_ref, bf16[128,8320]{1,0:T(8,128)(2,1)} %bitcast.8, f32[64,8320]{1,0:T(8,128)} %ctf_ref.1, f32[65,128]{1,0:T(8,128)} %bitcast.12, f32[16,128]{1,0:T(8,128)} %constant.2.clone.trig_ref, s32[4,2,4]{2,1,0:T(2,128)} %bitcast.13, ...), custom_call_target="tpu_custom_call" | custom-call | tf_op jit(solution)/shard_map/pallas_call | solution.py:521
  90.1 1.2 %slice_bitcast_fusion = f32[4]{0:T(128)} fusion(f32[8,128]{1,0:T(8,128)} %get-tuple-element.4), kind=kLoop, calls=%fused_computation | loop fusion | bytes 32 | tf_op jit(solution)/shard_map/squeeze | solution.py:567
  91.3 2.1 %copy.11 = f32[8,2,8320]{2,1,0:T(2,128)} copy(f32[8,2,8320]{2,0,1:T(8,128)} %bitcast.10) | data formatting | bytes 1064960

commit v5 on v3

--- a/solution.py
+++ b/solution.py
@@ -18,9 +18,9 @@
 HALF = TILES * LANES
 SHIFT = 32 * LANES
 HALF_A = 17 * LANES
-CHUNKS = 11
-CHUNK_TILES = TILES // CHUNKS
-CW = CHUNK_TILES * 2 * LANES
+SIZES = (5, 7, 8, 8, 5)
+STARTS = (0, 5, 12, 20, 28, 33)
+CHUNKS = len(SIZES)
 OTHERS = [(dz, dy) for dz in range(NZ) for dy in range(NY) if (dz, dy) != (0, 0)]
 F32 = jnp.float32
 BF16 = jnp.bfloat16
@@ -169,20 +169,6 @@
     lax.fori_loop(0, TILES, fill_rows, 0)
     top_row = lax.shift_right_logical((32 * core * LANES + lane) * 64528, 22)
 
-    for copy in meta_copies:
-        copy.wait_recv()
-
-    lane2 = lax.broadcasted_iota(jnp.int32, (8, 256), 1)
-
-    def fill_onehot(b, carry):
-        classes = smeta[b].astype(F32)[0:8, 8:9].astype(jnp.int32)
-        hit = jnp.logical_and(lane2 % 64 == classes, lane2 < 192)
-        onehot[pl.ds(pl.multiple_of(b * 8, 8), 8), :] = hit.astype(F32)
-        return carry
-
-    lax.fori_loop(0, BLOCKS, fill_onehot, 0)
-    ctf_copy.wait()
-
     def pieces(value):
         one = value.astype(BF16)
         rest = value - one.astype(F32)
@@ -191,7 +177,7 @@
         return one, two, three
 
     def fill_ctf(s, carry):
-        cols = pl.ds(pl.multiple_of(s * 384, 384), 384)
+        cols = pl.ds(pl.multiple_of(s * 1408, 1408), 1408)
         one, two, three = pieces(ctfh[:, cols])
         ctfrows[:, cols] = jnp.dot(
             onehot[...].astype(BF16),
@@ -200,27 +186,32 @@
         )
         return carry
 
-    lax.fori_loop(0, TILES // 3, fill_ctf, 0)
-
-    def weigh(s, total):
-        cols = pl.ds(pl.multiple_of(s * LANES, LANES), LANES)
-        first_ = praw[0, :, cols].astype(F32).reshape(2, 8, 1, 8, LANES)
-        second_ = praw[1, :, cols].astype(F32).reshape(2, 8, 1, 8, LANES)
-        both = jnp.concatenate([first_, second_], axis=2).reshape(2, 128, LANES)
-        counted = 1 - core * (1 - jnp.minimum(s, 1))
-        noise = noise_ref[pl.ds(core * 32 + s, 1), :] * counted.astype(F32)
-        scaled = (both * noise[None]).astype(BF16)
-        weights[pl.ds(pl.multiple_of(s * 256, 256), LANES), :] = scaled[0].T
-        weights[pl.ds(pl.multiple_of(s * 256 + 128, 128), LANES), :] = scaled[1].T
-        power = (both[0] * both[0] + both[1] * both[1]).T
-        ctf = ctfh[:, cols]
-        p1, p2, p3 = pieces(power)
-        c1, c2, c3 = pieces(ctf * ctf * noise)
-        return total + jnp.dot(
-            jnp.concatenate([c1, c1, c1, c2, c2, c3], axis=1),
-            jnp.concatenate([p1, p2, p3, p1, p2, p1], axis=0),
-            preferred_element_type=F32,
-        )
+
+    def weigh(n, total):
+        wide = pl.ds(pl.multiple_of(n * 384, 384), 384)
+        raw = [praw[0, :, wide], praw[1, :, wide]]
+        ctfs = ctfh[:, wide]
+        noises = [noise_ref[pl.ds(core * 32 + 3 * n + i, 1), :] for i in range(3)]
+        counted = 1 - core * (1 - jnp.minimum(n, 1))
+        noises[0] = noises[0] * counted.astype(F32)
+        turned = []
+        for i in range(3):
+            tile = slice(i * LANES, (i + 1) * LANES)
+            parts = [r[:, tile].astype(F32).reshape(2, 8, 1, 8, LANES) for r in raw]
+            both = jnp.concatenate(parts, axis=2).reshape(2, 128, LANES)
+            scaled = (both * noises[i][None]).astype(BF16)
+            turned += [scaled[0].T, scaled[1].T]
+            power = (both[0] * both[0] + both[1] * both[1]).T
+            ctf = ctfs[:, tile]
+            p1, p2, p3 = pieces(power)
+            c1, c2, c3 = pieces(ctf * ctf * noises[i])
+            total = total + jnp.dot(
+                jnp.concatenate([c1, c1, c1, c2, c2, c3], axis=1),
+                jnp.concatenate([p1, p2, p3, p1, p2, p1], axis=0),
+                preferred_element_type=F32,
+            )
+        weights[pl.ds(pl.multiple_of(n * 768, 768), 768), :] = jnp.concatenate(turned, axis=0)
+        return total
 
     cosine = trig_ref[0:8, :]
     sine = trig_ref[8:16, :]
@@ -244,31 +235,37 @@
             one_row.append(wave(slope))
             two_rows.append(wave(2 * slope))
 
-        def body(s, phases):
-            cols = pl.ds(pl.multiple_of(s * LANES, LANES), LANES)
-            block = gath[b, :, cols].astype(F32)
-            ctf = ctfrows[pl.ds(pl.multiple_of(b * 8, 8), 8), cols]
-            real, imag = block[0:8] * ctf, block[8:16] * ctf
-            single = vtab[s] == 1
-            reals, imags, later = [], [], []
-            for t in range(TRANS):
-                c, si = phases[t]
-                reals.append(real * c + imag * si)
-                imags.append(imag * c - real * si)
-                mc = jnp.where(single, one_row[t][0], two_rows[t][0])
-                ms = jnp.where(single, one_row[t][1], two_rows[t][1])
-                later.append((c * mc - si * ms, si * mc + c * ms))
+        def body(n, phases):
+            wide = pl.ds(pl.multiple_of(n * 384, 384), 384)
+            blocks = gath[b, :, wide].astype(F32)
+            ctfs = ctfrows[pl.ds(pl.multiple_of(b * 8, 8), 8), wide]
+            singles = [vtab[3 * n + i] == 1 for i in range(3)]
+            rows = [[], []]
+            for i in range(3):
+                tile = slice(i * LANES, (i + 1) * LANES)
+                ctf = ctfs[:, tile]
+                real, imag = blocks[0:8, tile] * ctf, blocks[8:16, tile] * ctf
+                reals, imags, later = [], [], []
+                for t in range(TRANS):
+                    c, si = phases[t]
+                    reals.append(real * c + imag * si)
+                    imags.append(imag * c - real * si)
+                    mc = jnp.where(singles[i], one_row[t][0], two_rows[t][0])
+                    ms = jnp.where(singles[i], one_row[t][1], two_rows[t][1])
+                    later.append((c * mc - si * ms, si * mc + c * ms))
+                phases = tuple(later)
+                for h in range(2):
+                    for values in (reals, imags):
+                        pair_ = jnp.concatenate(values[2 * h : 2 * h + 2], axis=0)
+                        rows[h].append(pair_.astype(BF16))
             for h in range(2):
                 at = pl.ds(pl.multiple_of(b * 32 + h * 16, 16), 16)
-                prep[at, pl.ds(pl.multiple_of(s * 256, 256), LANES)] = jnp.concatenate(
-                    reals[2 * h : 2 * h + 2], axis=0
-                ).astype(BF16)
-                prep[at, pl.ds(pl.multiple_of(s * 256 + 128, 128), LANES)] = jnp.concatenate(
-                    imags[2 * h : 2 * h + 2], axis=0
-                ).astype(BF16)
-            return tuple(later)
-
-        lax.fori_loop(0, TILES, body, tuple(begin), unroll=11)
+                prep[at, pl.ds(pl.multiple_of(n * 768, 768), 768)] = jnp.concatenate(
+                    rows[h], axis=1
+                )
+            return phases
+
+        lax.fori_loop(0, TILES // 3, body, tuple(begin), unroll=11)
 
     def score_group(g):
         rows = pl.ds(pl.multiple_of(g * 128, 128), 128)
@@ -325,14 +322,32 @@
 
         lax.fori_loop(0, 3, three, 0)
 
+    ctf_copy.wait()
+    proj_copy.wait()
+    praw_copy.wait_recv()
+    half_norms = lax.fori_loop(0, 4, weigh, jnp.zeros((64, 128), F32))
+
+    for copy in meta_copies:
+        copy.wait_recv()
+
+    lane2 = lax.broadcasted_iota(jnp.int32, (8, 256), 1)
+
+    def fill_onehot(b, carry):
+        classes = smeta[b].astype(F32)[0:8, 8:9].astype(jnp.int32)
+        hit = jnp.logical_and(lane2 % 64 == classes, lane2 < 192)
+        onehot[pl.ds(pl.multiple_of(b * 8, 8), 8), :] = hit.astype(F32)
+        return carry
+
+    lax.fori_loop(0, BLOCKS, fill_onehot, 0)
+    lax.fori_loop(0, 3, fill_ctf, 0)
+
     arrive(1)
     forward(0)
+    half_norms = lax.fori_loop(4, 8, weigh, half_norms)
+    arrive(2)
     prepare_three(0)
-    arrive(2)
     forward(1)
-    proj_copy.wait()
-    praw_copy.wait_recv()
-    norms[...] = 0.5 * lax.fori_loop(0, TILES, weigh, jnp.zeros((64, 128), F32), unroll=3)
+    norms[...] = 0.5 * lax.fori_loop(8, 11, weigh, half_norms)
     arrive(3)
     prepare_three(1)
     forward(2)
@@ -384,38 +399,35 @@
         ).astype(BF16)
 
     def copy_a(c):
-        return send(part.at[c, 2 * x2], from_a.at[c], a_s.at[c], a_r.at[c], right)
+        return send(part[c].at[2 * x2], from_a[c], a_s.at[c], a_r.at[c], right)
 
     def copy_b(c):
-        return send(part.at[c, 2 * x2 + 1], from_b.at[c], b_s.at[c], b_r.at[c], left)
+        return send(part[c].at[2 * x2 + 1], from_b[c], b_s.at[c], b_r.at[c], left)
 
     def copy_p(c):
-        return send(part.at[c, pl.ds(2 * xp, 2)], from_p.at[c], p_s.at[c], p_r.at[c], right)
+        return send(part[c].at[pl.ds(2 * xp, 2)], from_p[c], p_s.at[c], p_r.at[c], right)
 
     def copy_m(c):
-        return send(part.at[c, pl.ds(2 * xm, 2)], from_m.at[c], m_s.at[c], m_r.at[c], left)
+        return send(part[c].at[pl.ds(2 * xm, 2)], from_m[c], m_s.at[c], m_r.at[c], left)
 
     def copy_w(c, k):
-        return send(zsend.at[c, k], zrecv.at[c, core], w_s.at[c, k], w_r.at[c, core], across[k])
+        return send(
+            zsend[c].at[k], zrecv[c].at[core], w_s.at[c, k], w_r.at[c, core], across[k]
+        )
 
     def arrived_w(c, half):
-        return send(zsend.at[c, 0], zrecv.at[c, half], w_s.at[c, 0], w_r.at[c, half], across[0])
+        return send(zsend[c].at[0], zrecv[c].at[half], w_s.at[c, 0], w_r.at[c, half], across[0])
 
     def copy_f(c):
         other = pl.ds(pl.multiple_of((1 - core) * 8, 8), 8)
-        return send(keep.at[c, other], fin.at[c], f_s.at[c], f_r.at[c], peer)
-
-    def write(c, half, value):
-        for s in range(CHUNK_TILES):
-            at = pl.ds(pl.multiple_of(half * SHIFT + (c * CHUNK_TILES + s) * LANES, LANES), LANES)
-            for k in range(2):
-                out_ref[k, :, at] = value[:, s * 256 + k * 128 : s * 256 + k * 128 + 128]
+        return send(keep[c].at[other], fin[c], f_s.at[c], f_r.at[c], peer)
 
     def project(c):
-        cols = pl.ds(pl.multiple_of(c * CW, CW), CW)
-        sums = jnp.dot(post[...], prep[:, cols], preferred_element_type=F32).astype(BF16)
+        sums = jnp.dot(
+            post[...], prep[:, STARTS[c] * 256 : STARTS[c + 1] * 256], preferred_element_type=F32
+        ).astype(BF16)
         for i in range(8):
-            part[c, i] = sums[16 * i : 16 * i + 16]
+            part[c][i] = sums[16 * i : 16 * i + 16]
         copy_a(c).start()
         copy_b(c).start()
 
@@ -427,46 +439,44 @@
 
     def pass_on(c):
         copy_a(c).wait_recv()
-        part[c, 2 * xp] = add(part[c, 2 * xp], from_a[c]).astype(BF16)
+        part[c][2 * xp] = add(part[c][2 * xp], from_a[c][...]).astype(BF16)
         copy_p(c).start()
         copy_b(c).wait_recv()
-        part[c, 2 * xm + 1] = add(part[c, 2 * xm + 1], from_b[c]).astype(BF16)
+        part[c][2 * xm + 1] = add(part[c][2 * xm + 1], from_b[c][...]).astype(BF16)
         copy_m(c).start()
 
     def collect(c):
+        half = SIZES[c] * LANES
         copy_p(c).wait_recv()
         copy_m(c).wait_recv()
         far = 1 - zh
-        away = add(part[c, 2 * x + far], from_p[c, far], from_m[c, far])
+        away = add(part[c][2 * x + far], from_p[c][far], from_m[c][far])
         for k in range(2):
             rows = away[8 * k : 8 * k + 8]
-            zsend[c, k] = jnp.concatenate([rows[:, : CW // 2], rows[:, CW // 2 :]], axis=0).astype(BF16)
+            zsend[c][k] = jnp.concatenate([rows[:, :half], rows[:, half:]], axis=0).astype(BF16)
             copy_w(c, k).start()
-        keep[c] = add(part[c, 2 * x + zh], from_p[c, zh], from_m[c, zh])
+        keep[c][...] = add(part[c][2 * x + zh], from_p[c][zh], from_m[c][zh])
         copy_f(c).start()
 
     def complete(c):
         for half in range(2):
             arrived_w(c, half).wait_recv()
         copy_f(c).wait_recv()
-        here = keep[c, pl.ds(pl.multiple_of(core * 8, 8), 8), :]
-        for half, near in ((core, here), (1 - core, fin[c])):
-            rows = zrecv[c, half].astype(F32)
-            write(c, half, near + jnp.concatenate([rows[0:8], rows[8:16]], axis=1))
-
-    stages = [(0, project), (3, pass_on), (6, collect), (10, complete)]
-
-    def step(n, carry):
-        for lag, stage in stages:
-            here = jnp.logical_and(n >= lag, n < CHUNKS + lag)
-
-            @pl.when(here)
-            def _(lag=lag, stage=stage):
+        here = keep[c][pl.ds(pl.multiple_of(core * 8, 8), 8), :]
+        for half, near in ((core, here), (1 - core, fin[c][...])):
+            rows = zrecv[c][half].astype(F32)
+            value = near + jnp.concatenate([rows[0:8], rows[8:16]], axis=1)
+            for s in range(SIZES[c]):
+                at = pl.multiple_of(half * SHIFT + (STARTS[c] + s) * LANES, LANES)
+                for k in range(2):
+                    out_ref[k, :, pl.ds(at, LANES)] = value[
+                        :, s * 256 + k * 128 : s * 256 + k * 128 + 128
+                    ]
+
+    for n in range(CHUNKS + 4):
+        for lag, stage in ((0, project), (1, pass_on), (2, collect), (4, complete)):
+            if 0 <= n - lag < CHUNKS:
                 stage(n - lag)
-
-        return carry
-
-    lax.fori_loop(0, CHUNKS + 10, step, 0)
 
     pmeta_copy.wait_send()
     pair_copy.wait_send()
@@ -477,14 +487,11 @@
         pl.when(goes_right[q])(lambda q=q: z_right[q].wait_send())
         pl.when(goes_left[q])(lambda q=q: z_left[q].wait_send())
 
-    def sent(c, carry):
+    for c in range(CHUNKS):
         for copy in (copy_a, copy_b, copy_p, copy_m, copy_f):
             copy(c).wait_send()
         for k in range(2):
             copy_w(c, k).wait_send()
-        return carry
-
-    lax.fori_loop(0, CHUNKS, sent, 0)
 
 
 def per_device(images, projections, ctf_table, noise_weight, shifts, defocus):
@@ -528,15 +535,15 @@
             pltpu.VMEM((4, 128, 128), F32),
             pltpu.VMEM((BLOCKS, 16, LANES), F32),
             pltpu.VMEM((128, 512), BF16),
-            pltpu.VMEM((CHUNKS, 8, 16, CW), BF16),
-            pltpu.VMEM((CHUNKS, 16, CW), BF16),
-            pltpu.VMEM((CHUNKS, 16, CW), BF16),
-            pltpu.VMEM((CHUNKS, 2, 16, CW), BF16),
-            pltpu.VMEM((CHUNKS, 2, 16, CW), BF16),
-            pltpu.VMEM((CHUNKS, 2, 16, CW // 2), BF16),
-            pltpu.VMEM((CHUNKS, 2, 16, CW // 2), BF16),
-            pltpu.VMEM((CHUNKS, 16, CW), F32),
-            pltpu.VMEM((CHUNKS, 8, CW), F32),
+            [pltpu.VMEM((8, 16, 256 * t), BF16) for t in SIZES],
+            [pltpu.VMEM((16, 256 * t), BF16) for t in SIZES],
+            [pltpu.VMEM((16, 256 * t), BF16) for t in SIZES],
+            [pltpu.VMEM((2, 16, 256 * t), BF16) for t in SIZES],
+            [pltpu.VMEM((2, 16, 256 * t), BF16) for t in SIZES],
+            [pltpu.VMEM((2, 16, 128 * t), BF16) for t in SIZES],
+            [pltpu.VMEM((2, 16, 128 * t), BF16) for t in SIZES],
+            [pltpu.VMEM((16, 256 * t), F32) for t in SIZES],
+            [pltpu.VMEM((8, 256 * t), F32) for t in SIZES],
             *sems,
         ],
         compiler_params=pltpu.CompilerParams(

time: 89.7 us -> 85.3 us (0.951)
  Pallas kernels: 80.7 us -> 76.3 us
    pallas_call x1, Pallas kernels: 80.7 us -> 76.3 us  [per_device(): pl.pallas_call(kernel, out_shape=(jax.ShapeDtypeStruct((2, 8, pixels), F3...]
where the time goes in v5:
time: 85.3 us; the launch traced here: 85.1 us
  Pallas kernels  76.3 us (89%)
  local copies, waits for them, and re-layouts  8.1 us (9%)
    pallas_call x1, Pallas kernels, per_device(): pl.pallas_call(kernel, out_shape=(jax.ShapeDtypeStruct((2, 8, pixels), F3...  76.3 us
    transpose x1, local copies, waits for them, and re-layouts, per_device(): proj = projections.transpose(1, 0, 2).reshape(128, pixels)  3.15 us
    unnamed x1, local copies, waits for them, and re-layouts  2.11 us

profile of v5, /device:TPU:1, one launch (start us, length us, event | category | flops | bytes accessed | tf_op | source)
XLA Modules:
  0.0 85.1 jit_solution(14185293666883596479)
XLA Ops:
  0.6 1.0 %copy.9 = bf16[2,4,8320]{2,1,0:T(4,128)(2,1)S(1)} copy(bf16[2,4,8320]{2,0,1:T(2,128)(2,1)} %bitcast.11) | data formatting | bytes 266240 | tf_op jit(solution)/shard_map/transpose | solution.py:500
  1.6 0.7 reshape.13.img_ref
  2.3 3.2 %copy.10 = bf16[2,64,8320]{2,1,0:T(8,128)(2,1)} copy(bf16[2,64,8320]{2,0,1:T(2,128)(2,1)} %bitcast.9) | data formatting | bytes 4259840 | tf_op jit(solution)/shard_map/transpose | solution.py:501
  5.4 76.3 %shard_map.86 = (f32[2,8,8320]{2,1,0:T(8,128)}, f32[8,128]{1,0:T(8,128)}) custom-call(bf16[8,8320]{1,0:T(8,128)(2,1)} %reshape.13.img_ref, bf16[128,8320]{1,0:T(8,128)(2,1)} %bitcast.8, f32[64,8320]{1,0:T(8,128)} %ctf_ref.1, f32[65,128]{1,0:T(8,128)} %bitcast.12, f32[16,128]{1,0:T(8,128)} %constant.2.clone.trig_ref, s32[4,2,4]{2,1,0:T(2,128)} %bitcast.13, ...), custom_call_target="tpu_custom_call" | custom-call | tf_op jit(solution)/shard_map/pallas_call | solution.py:511
  81.8 1.2 %slice_bitcast_fusion = f32[4]{0:T(128)} fusion(f32[8,128]{1,0:T(8,128)} %get-tuple-element.4), kind=kLoop, calls=%fused_computation | loop fusion | bytes 32 | tf_op jit(solution)/shard_map/squeeze | solution.py:556
  82.9 2.1 %copy.11 = f32[8,2,8320]{2,1,0:T(2,128)} copy(f32[8,2,8320]{2,0,1:T(8,128)} %bitcast.10) | data formatting | bytes 1064960

commit v6 on v5

--- a/solution.py
+++ b/solution.py
@@ -73,20 +73,21 @@
 
     lane = lax.broadcasted_iota(jnp.int32, (8, LANES), 1)
     place = lax.broadcasted_iota(jnp.int32, (8, LANES), 0)
-    held_here = (place >= 4) == (core == 1)
 
     def lay_out(s, carry):
-        cols = pl.ds(pl.multiple_of(s * LANES, LANES), LANES)
-        straight = img_ref[:, cols].astype(F32)
-        swapped = pltpu.roll(straight, 4, 0)
-        low = jnp.where(core == 0, straight, swapped)
-        high = jnp.where(core == 0, swapped, straight)
-        both = jnp.concatenate([low, high], axis=0)
-        seen = jnp.concatenate([held_here, held_here], axis=0)
-        placed[:, cols] = jnp.where(seen, both, 0.0).astype(BF16)
+        cols = pl.ds(pl.multiple_of(s * 5 * LANES, LANES), 5 * LANES)
+        at = lax.broadcasted_iota(jnp.int32, (8, 5 * LANES), 0)
+        real = jnp.zeros((8, 5 * LANES), F32)
+        imag = jnp.zeros((8, 5 * LANES), F32)
+        for i in range(4):
+            both = img_ref[i, :, cols].astype(F32)
+            here = at == i + 4 * core
+            real = jnp.where(here, both[0:1], real)
+            imag = jnp.where(here, both[1:2], imag)
+        placed[:, cols] = jnp.concatenate([real, imag], axis=0).astype(BF16)
         return carry
 
-    lax.fori_loop(0, 65, lay_out, 0, unroll=5)
+    lax.fori_loop(0, 13, lay_out, 0)
     meta = jnp.zeros((8, LANES), jnp.int32)
     for i in range(4):
         row = place == i + 4 * core
@@ -391,8 +392,9 @@
     total = total + turn(total, 8)
     total = total + turn(total, 16)
     evidence = largest + jnp.log(total)
-    own_row = jnp.sum(jnp.where(place == zl, evidence, 0.0), axis=0, keepdims=True)
-    ev_ref[...] = pltpu.roll(jnp.broadcast_to(own_row, (8, LANES)), 128 - (y * 32 + core * 4), 1)
+    for i in range(4):
+        spot = jnp.logical_and(place == zl, lane == y * 32 + core * 4 + i)
+        ev_ref[i] = jnp.sum(jnp.where(spot, evidence, 0.0))
     for g in range(4):
         post[:, g * 128 : (g + 1) * 128] = (
             jnp.exp(pscore[g] - evidence[g : g + 1, :]) * 2048.0
@@ -469,7 +471,7 @@
             for s in range(SIZES[c]):
                 at = pl.multiple_of(half * SHIFT + (STARTS[c] + s) * LANES, LANES)
                 for k in range(2):
-                    out_ref[k, :, pl.ds(at, LANES)] = value[
+                    out_ref[:, k, pl.ds(at, LANES)] = value[
                         :, s * 256 + k * 128 : s * 256 + k * 128 + 128
                     ]
 
@@ -497,7 +499,6 @@
 def per_device(images, projections, ctf_table, noise_weight, shifts, defocus):
     local = images.shape[0]
     pixels = images.shape[2]
-    rows = images.transpose(1, 0, 2).reshape(2 * local, pixels)
     proj = projections.transpose(1, 0, 2).reshape(128, pixels)
     angles = np.arange(KY) * (2.0 * math.pi / KY)
     trig = np.concatenate([np.tile(np.cos(angles), (8, 1)), np.tile(np.sin(angles), (8, 1))])
@@ -511,11 +512,11 @@
     sums, evidence = pl.pallas_call(
         kernel,
         out_shape=(
-            jax.ShapeDtypeStruct((2, 8, pixels), F32),
-            jax.ShapeDtypeStruct((8, LANES), F32),
+            jax.ShapeDtypeStruct((8, 2, pixels), F32),
+            jax.ShapeDtypeStruct((local,), F32),
         ),
         in_specs=[vmem, hbm, hbm, vmem, vmem, smem, smem],
-        out_specs=(vmem, vmem),
+        out_specs=(vmem, smem),
         scratch_shapes=[
             pltpu.VMEM((16, 65 * LANES), BF16),
             pltpu.VMEM((16, LANES), BF16),
@@ -550,10 +551,10 @@
             collective_id=0, has_side_effects=True, vmem_limit_bytes=56 * 1024 * 1024
         ),
     )(
-        rows, proj, ctf_table, noise_weight.reshape(65, LANES), trig,
+        images, proj, ctf_table, noise_weight.reshape(65, LANES), trig,
         shifts.transpose(0, 2, 1), defocus,
     )
-    return evidence[0, :local], sums.transpose(1, 0, 2)
+    return evidence, sums
 
 
 def solution(mesh):

time: 85.3 us -> 83.4 us (0.978)
  local copies, waits for them, and re-layouts: 8.1 us -> 6.22 us
    squeeze x1 -> x0, local copies, waits for them, and re-layouts: 1.19 us -> none  [per_device(): return (evidence[0, :local], sums.transpose(1, 0, 2))]
    transpose x1 -> x0, local copies, waits for them, and re-layouts: 0.96 us -> none  [per_device(): rows = images.transpose(1, 0, 2).reshape(2 * local, pixels)]
    unnamed x1 -> x2, local copies, waits for them, and re-layouts: 2.11 us -> 3.06 us
where the time goes in v6:
time: 83.4 us; the launch traced here: 83.2 us
  Pallas kernels  76.4 us (92%)
  local copies, waits for them, and re-layouts  6.22 us (7%)
    pallas_call x1, Pallas kernels, per_device(): pl.pallas_call(kernel, out_shape=(jax.ShapeDtypeStruct((8, 2, pixels), F3...  76.4 us
    transpose x1, local copies, waits for them, and re-layouts, per_device(): proj = projections.transpose(1, 0, 2).reshape(128, pixels)  3.16 us
    unnamed x2, local copies, waits for them, and re-layouts  3.06 us

profile of v6, /device:TPU:1, one launch (start us, length us, event | category | flops | bytes accessed | tf_op | source)
XLA Modules:
  0.0 83.2 jit_solution(17342741460356478428)
XLA Ops:
  0.6 3.2 %copy.9 = bf16[2,64,8320]{2,1,0:T(8,128)(2,1)} copy(bf16[2,64,8320]{2,0,1:T(2,128)(2,1)} %bitcast.5) | data formatting | bytes 4259840 | tf_op jit(solution)/shard_map/transpose | solution.py:502
  3.8 76.4 %shard_map.86 = (f32[8,2,8320]{2,1,0:T(2,128)}, f32[4]{0:T(128)}) custom-call(bf16[4,2,8320]{2,1,0:T(2,128)(2,1)} %img_ref.1, bf16[128,8320]{1,0:T(8,128)(2,1)} %bitcast.4, f32[64,8320]{1,0:T(8,128)} %ctf_ref.1, f32[65,128]{1,0:T(8,128)} %bitcast.6, f32[16,128]{1,0:T(8,128)} %constant.2.clone.trig_ref, s32[4,2,4]{2,1,0:T(2,128)} %bitcast.7, s32[4]{0:T(128)} %class_ref.1), custom_call_target="tpu_custom_call" | custom-call | tf_op jit(solution)/shard_map/pallas_call | solution.py:512
  80.2 1.2 %copy.12 = f32[4]{0:T(128)} copy(f32[4]{0:T(128)} %get-tuple-element.8) | data formatting | bytes 32
  81.4 1.9 %copy.13 = f32[8,2,8320]{2,1,0:T(2,128)} copy(f32[8,2,8320]{2,1,0:T(2,128)} %get-tuple-element.9) | data formatting | bytes 1064960

commit v7 on v6

--- a/solution.py
+++ b/solution.py
@@ -22,6 +22,9 @@
 STARTS = (0, 5, 12, 20, 28, 33)
 CHUNKS = len(SIZES)
 OTHERS = [(dz, dy) for dz in range(NZ) for dy in range(NY) if (dz, dy) != (0, 0)]
+ORDERS = ((0, 1, 2, 3), (1, 0, 2, 3), (2, 3, 1, 0), (3, 2, 1, 0))
+STEP_OF = (0, 0, 0, 1, 1, 1, 0, 2, 2, 2, 1, 3, 3, 3, 2, 3)
+AHEAD_OF = (3, 0, 1, 3, 0, 1, 2, 3, 0, 1, 2, 3, 0, 1, 2, 2)
 F32 = jnp.float32
 BF16 = jnp.bfloat16
 HI = lax.Precision.HIGHEST
@@ -127,7 +130,7 @@
         high = (1 - b0) * table[2] + b0 * table[3]
         return (1 - b1) * low + b1 * high
 
-    order = [zl, pick([1, 0, 3, 2]), pick([2, 2, 1, 1]), pick([3, 3, 0, 0])]
+    order = [pick([row[q] for row in ORDERS]) for q in range(4)]
 
     def z_copy(zq, step, target):
         b = zq * 4 + y
@@ -188,7 +191,8 @@
         return carry
 
 
-    def weigh(n, total):
+    def weigh(n):
+        total = norms[...]
         wide = pl.ds(pl.multiple_of(n * 384, 384), 384)
         raw = [praw[0, :, wide], praw[1, :, wide]]
         ctfs = ctfh[:, wide]
@@ -205,14 +209,14 @@
             power = (both[0] * both[0] + both[1] * both[1]).T
             ctf = ctfs[:, tile]
             p1, p2, p3 = pieces(power)
-            c1, c2, c3 = pieces(ctf * ctf * noises[i])
+            c1, c2, c3 = pieces(0.5 * ctf * ctf * noises[i])
             total = total + jnp.dot(
                 jnp.concatenate([c1, c1, c1, c2, c2, c3], axis=1),
                 jnp.concatenate([p1, p2, p3, p1, p2, p1], axis=0),
                 preferred_element_type=F32,
             )
         weights[pl.ds(pl.multiple_of(n * 768, 768), 768), :] = jnp.concatenate(turned, axis=0)
-        return total
+        norms[...] = total
 
     cosine = trig_ref[0:8, :]
     sine = trig_ref[8:16, :]
@@ -283,29 +287,26 @@
         norm = jnp.dot(picked[:, :64], norms[...], precision=HI, preferred_element_type=F32)
         score[g] = cross - norm
 
-    sc_copies = [
-        send(score.at[order[q]], pscore.at[order[q]], sc_s.at[q], sc_r.at[q], peer)
-        for q in range(4)
-    ]
+    packed = pick([sum(o << (2 * k) for k, o in enumerate(row)) for row in ORDERS])
+
+    def order_at(q):
+        return lax.shift_right_logical(packed, 2 * q) & 3
+
+    def sc_copy(q):
+        g = order_at(q)
+        return send(score.at[g], pscore.at[g], sc_s.at[q], sc_r.at[q], peer)
 
     stats[own] = jnp.zeros((16, LANES), F32)
 
     def summarise(q):
-        sc_copies[q].wait_recv()
-        g = order[q]
+        sc_copy(q).wait_recv()
+        g = order_at(q)
         whole = (score[g] + pscore[g]).T
         pscore[g] = whole
         top = jnp.max(whole, axis=0, keepdims=True)
         stats[own, pl.ds(g, 1), :] = top
         stats[own, pl.ds(8 + g, 1), :] = jnp.sum(jnp.exp(whole - top), axis=0, keepdims=True)
 
-    def finish(q):
-        fwd_up[q].wait_recv()
-        fwd_down[q].wait_recv()
-        prepare(order[q] * 4 + y2)
-        score_group(order[q])
-        sc_copies[q].start()
-
     def arrive(q):
         z_right[q].wait_recv()
         launch(q)
@@ -316,52 +317,67 @@
         y_down[q].wait_recv()
         fwd_down[q].start()
 
-    def prepare_three(q):
-        def three(i, carry):
-            prepare(order[q] * 4 + (y + 3 + i) % 4)
+    def know():
+        for copy in meta_copies:
+            copy.wait_recv()
+        lane2 = lax.broadcasted_iota(jnp.int32, (8, 256), 1)
+
+        def fill_onehot(b, carry):
+            classes = smeta[b].astype(F32)[0:8, 8:9].astype(jnp.int32)
+            hit = jnp.logical_and(lane2 % 64 == classes, lane2 < 192)
+            onehot[pl.ds(pl.multiple_of(b * 8, 8), 8), :] = hit.astype(F32)
             return carry
 
-        lax.fori_loop(0, 3, three, 0)
+        lax.fori_loop(0, BLOCKS, fill_onehot, 0)
+        lax.fori_loop(0, 3, fill_ctf, 0)
 
     ctf_copy.wait()
     proj_copy.wait()
     praw_copy.wait_recv()
-    half_norms = lax.fori_loop(0, 4, weigh, jnp.zeros((64, 128), F32))
-
-    for copy in meta_copies:
-        copy.wait_recv()
-
-    lane2 = lax.broadcasted_iota(jnp.int32, (8, 256), 1)
-
-    def fill_onehot(b, carry):
-        classes = smeta[b].astype(F32)[0:8, 8:9].astype(jnp.int32)
-        hit = jnp.logical_and(lane2 % 64 == classes, lane2 < 192)
-        onehot[pl.ds(pl.multiple_of(b * 8, 8), 8), :] = hit.astype(F32)
+    norms[...] = jnp.zeros((64, 128), F32)
+
+    def weighing(n, carry):
+        @pl.when(n == 4)
+        def _():
+            know()
+            arrive(1)
+            forward(0)
+
+        pl.when(n == 8)(lambda: arrive(2))
+        weigh(n)
         return carry
 
-    lax.fori_loop(0, BLOCKS, fill_onehot, 0)
-    lax.fori_loop(0, 3, fill_ctf, 0)
-
-    arrive(1)
-    forward(0)
-    half_norms = lax.fori_loop(4, 8, weigh, half_norms)
-    arrive(2)
-    prepare_three(0)
-    forward(1)
-    norms[...] = 0.5 * lax.fori_loop(8, 11, weigh, half_norms)
-    arrive(3)
-    prepare_three(1)
-    forward(2)
-    finish(0)
-    prepare_three(2)
-    forward(3)
-    finish(1)
-    summarise(0)
-    prepare_three(3)
-    finish(2)
-    summarise(1)
-    finish(3)
-    summarise(2)
+    lax.fori_loop(0, TILES // 3, weighing, 0)
+
+    def look_up(table, n):
+        low, high = (sum(v << (2 * k) for k, v in enumerate(table[i : i + 8])) for i in (0, 8))
+        return lax.shift_right_logical(low + (n // 8) * (high - low), 2 * (n % 8)) & 3
+
+    def blocks(n, carry):
+        q, ahead = look_up(STEP_OF, n), look_up(AHEAD_OF, n)
+        pl.when(n == 1)(lambda: forward(1))
+        pl.when(n == 3)(lambda: arrive(3))
+        pl.when(n == 6)(lambda: forward(2))
+        pl.when(n == 10)(lambda: forward(3))
+
+        @pl.when(ahead == 2)
+        def _():
+            b = order_at(q) * 4 + y2
+            low, high = gath.at[b, :, first], gath.at[b, :, second]
+            send(low, low, fa_s.at[q], fa_r.at[q], up).wait_recv()
+            send(high, high, fb_s.at[q], fb_r.at[q], down).wait_recv()
+
+        prepare(order_at(q) * 4 + (y + ahead) % 4)
+
+        @pl.when(ahead == 2)
+        def _():
+            score_group(order_at(q))
+            sc_copy(q).start()
+            pl.when(q >= 1)(lambda: summarise(q - 1))
+
+        return carry
+
+    lax.fori_loop(0, BLOCKS, blocks, 0)
     summarise(3)
 
     stat_copies = [
@@ -483,7 +499,7 @@
     pmeta_copy.wait_send()
     pair_copy.wait_send()
     praw_copy.wait_send()
-    for copy in meta_copies + stat_copies + sc_copies + y_up + y_down + fwd_up + fwd_down:
+    for copy in meta_copies + stat_copies + [sc_copy(q) for q in range(4)] + y_up + y_down + fwd_up + fwd_down:
         copy.wait_send()
     for q in range(4):
         pl.when(goes_right[q])(lambda q=q: z_right[q].wait_send())

time: 83.4 us -> 84.5 us (1.013)
  Pallas kernels: 76.4 us -> 77.4 us
    pallas_call x1, Pallas kernels: 76.4 us -> 77.4 us  [per_device(): pl.pallas_call(kernel, out_shape=(jax.ShapeDtypeStruct((8, 2, pixels), F3...]
where the time goes in v7:
time: 84.5 us; the launch traced here: 84.3 us
  Pallas kernels  77.4 us (92%)
  local copies, waits for them, and re-layouts  6.22 us (7%)
    pallas_call x1, Pallas kernels, per_device(): pl.pallas_call(kernel, out_shape=(jax.ShapeDtypeStruct((8, 2, pixels), F3...  77.4 us
    transpose x1, local copies, waits for them, and re-layouts, per_device(): proj = projections.transpose(1, 0, 2).reshape(128, pixels)  3.16 us
    unnamed x2, local copies, waits for them, and re-layouts  3.06 us

profile of v7, /device:TPU:1, one launch (start us, length us, event | category | flops | bytes accessed | tf_op | source)
XLA Modules:
  0.0 84.3 jit_solution(5756442573227521607)
XLA Ops:
  0.6 3.2 %copy.9 = bf16[2,64,8320]{2,1,0:T(8,128)(2,1)} copy(bf16[2,64,8320]{2,0,1:T(2,128)(2,1)} %bitcast.5) | data formatting | bytes 4259840 | tf_op jit(solution)/shard_map/transpose | solution.py:518
  3.8 77.4 %shard_map.86 = (f32[8,2,8320]{2,1,0:T(2,128)}, f32[4]{0:T(128)}) custom-call(bf16[4,2,8320]{2,1,0:T(2,128)(2,1)} %img_ref.1, bf16[128,8320]{1,0:T(8,128)(2,1)} %bitcast.4, f32[64,8320]{1,0:T(8,128)} %ctf_ref.1, f32[65,128]{1,0:T(8,128)} %bitcast.6, f32[16,128]{1,0:T(8,128)} %constant.2.clone.trig_ref, s32[4,2,4]{2,1,0:T(2,128)} %bitcast.7, s32[4]{0:T(128)} %class_ref.1), custom_call_target="tpu_custom_call" | custom-call | tf_op jit(solution)/shard_map/pallas_call | solution.py:528
  81.2 1.2 %copy.12 = f32[4]{0:T(128)} copy(f32[4]{0:T(128)} %get-tuple-element.8) | data formatting | bytes 32
  82.4 1.9 %copy.13 = f32[8,2,8320]{2,1,0:T(2,128)} copy(f32[8,2,8320]{2,1,0:T(2,128)} %get-tuple-element.9) | data formatting | bytes 1064960

commit v8 on v6

--- a/solution.py
+++ b/solution.py
@@ -30,7 +30,7 @@
 def kernel(
     img_ref, proj_ref, ctf_ref, noise_ref, trig_ref, shift_ref, class_ref,
     out_ref, ev_ref,
-    placed, ometa, pair, pmeta, smeta, gath, praw, ctfh, weights, norms, onehot, ctfrows, vtab, prep,
+    placed, ometa, pair, pmeta, smeta, gath, praw, ctfh, weights, norms, normrows, onehot, ctfrows, vtab, prep,
     score, pscore, stats, post, part, from_a, from_b, from_p, from_m, zsend, zrecv, keep, fin,
     loc_sem, core_s, core_r, meta_s, meta_r, stat_s, stat_r, z_s, z_r,
     yp_s, ym_s, yl_r, yr_r, fa_s, fb_s, fa_r, fb_r, sc_s, sc_r,
@@ -236,7 +236,8 @@
             one_row.append(wave(slope))
             two_rows.append(wave(2 * slope))
 
-        def body(n, phases):
+        def body(n, carry):
+            phases, total = carry
             wide = pl.ds(pl.multiple_of(n * 384, 384), 384)
             blocks = gath[b, :, wide].astype(F32)
             ctfs = ctfrows[pl.ds(pl.multiple_of(b * 8, 8), 8), wide]
@@ -259,29 +260,17 @@
                     for values in (reals, imags):
                         pair_ = jnp.concatenate(values[2 * h : 2 * h + 2], axis=0)
                         rows[h].append(pair_.astype(BF16))
-            for h in range(2):
-                at = pl.ds(pl.multiple_of(b * 32 + h * 16, 16), 16)
-                prep[at, pl.ds(pl.multiple_of(n * 768, 768), 768)] = jnp.concatenate(
-                    rows[h], axis=1
-                )
-            return phases
-
-        lax.fori_loop(0, TILES // 3, body, tuple(begin), unroll=11)
-
-    def score_group(g):
-        rows = pl.ds(pl.multiple_of(g * 128, 128), 128)
-
-        def body(i, total):
-            cols = pl.ds(pl.multiple_of(i * 768, 768), 768)
-            return total + jnp.dot(
-                prep[rows, cols], weights[cols, :], preferred_element_type=F32
-            )
-
-        cross = lax.fori_loop(0, TILES // 3, body, jnp.zeros((128, 128), F32), unroll=11)
-        picked = onehot[pl.ds(pl.multiple_of(g * 32, 32), 32), 0:LANES].reshape(4, 1, 8, LANES)
-        picked = jnp.concatenate([picked] * TRANS, axis=1).reshape(128, LANES)
-        norm = jnp.dot(picked[:, :64], norms[...], precision=HI, preferred_element_type=F32)
-        score[g] = cross - norm
+            steps = pl.ds(pl.multiple_of(n * 768, 768), 768)
+            made = jnp.concatenate([jnp.concatenate(r, axis=1) for r in rows], axis=0)
+            total = total + jnp.dot(made, weights[steps, :], preferred_element_type=F32)
+            prep[pl.ds(pl.multiple_of(b * 32, 32), 32), steps] = made
+            return phases, total
+
+        start = (tuple(begin), jnp.zeros((32, LANES), F32))
+        _, cross = lax.fori_loop(0, TILES // 3, body, start, unroll=11)
+        norm = normrows[pl.ds(pl.multiple_of(b * 8, 8), 8), :]
+        at = pl.ds(pl.multiple_of((b % 4) * 32, 32), 32)
+        score[b // 4, at, :] = cross - jnp.concatenate([norm] * TRANS, axis=0)
 
     sc_copies = [
         send(score.at[order[q]], pscore.at[order[q]], sc_s.at[q], sc_r.at[q], peer)
@@ -303,7 +292,6 @@
         fwd_up[q].wait_recv()
         fwd_down[q].wait_recv()
         prepare(order[q] * 4 + y2)
-        score_group(order[q])
         sc_copies[q].start()
 
     def arrive(q):
@@ -344,11 +332,14 @@
 
     arrive(1)
     forward(0)
-    half_norms = lax.fori_loop(4, 8, weigh, half_norms)
+    half_norms = lax.fori_loop(4, 11, weigh, half_norms)
+    norms[...] = 0.5 * half_norms
+    normrows[...] = jnp.dot(
+        onehot[:, 0:64], norms[...], precision=HI, preferred_element_type=F32
+    )
     arrive(2)
     prepare_three(0)
     forward(1)
-    norms[...] = 0.5 * lax.fori_loop(8, 11, weigh, half_norms)
     arrive(3)
     prepare_three(1)
     forward(2)
@@ -528,6 +519,7 @@
             pltpu.VMEM((64, HALF), F32),
             pltpu.VMEM((2 * HALF, 128), BF16),
             pltpu.VMEM((64, 128), F32),
+            pltpu.VMEM((128, 128), F32),
             pltpu.VMEM((128, 2 * LANES), F32),
             pltpu.VMEM((128, HALF), F32),
             pltpu.VMEM((TILES, 8, LANES), jnp.int32),

time: 83.4 us -> 83.5 us (level)
  no operation moved by 1% of the time
where the time goes in v8:
time: 83.5 us; the launch traced here: 83.3 us
  Pallas kernels  76.4 us (91%)
  local copies, waits for them, and re-layouts  6.22 us (7%)
    pallas_call x1, Pallas kernels, per_device(): pl.pallas_call(kernel, out_shape=(jax.ShapeDtypeStruct((8, 2, pixels), F3...  76.4 us
    transpose x1, local copies, waits for them, and re-layouts, per_device(): proj = projections.transpose(1, 0, 2).reshape(128, pixels)  3.16 us
    unnamed x2, local copies, waits for them, and re-layouts  3.06 us

profile of v8, /device:TPU:1, one launch (start us, length us, event | category | flops | bytes accessed | tf_op | source)
XLA Modules:
  0.0 83.3 jit_solution(3040657874187512826)
XLA Ops:
  0.6 3.2 %copy.9 = bf16[2,64,8320]{2,1,0:T(8,128)(2,1)} copy(bf16[2,64,8320]{2,0,1:T(2,128)(2,1)} %bitcast.5) | data formatting | bytes 4259840 | tf_op jit(solution)/shard_map/transpose | solution.py:493
  3.8 76.4 %shard_map.86 = (f32[8,2,8320]{2,1,0:T(2,128)}, f32[4]{0:T(128)}) custom-call(bf16[4,2,8320]{2,1,0:T(2,128)(2,1)} %img_ref.1, bf16[128,8320]{1,0:T(8,128)(2,1)} %bitcast.4, f32[64,8320]{1,0:T(8,128)} %ctf_ref.1, f32[65,128]{1,0:T(8,128)} %bitcast.6, f32[16,128]{1,0:T(8,128)} %constant.2.clone.trig_ref, s32[4,2,4]{2,1,0:T(2,128)} %bitcast.7, s32[4]{0:T(128)} %class_ref.1), custom_call_target="tpu_custom_call" | custom-call | tf_op jit(solution)/shard_map/pallas_call | solution.py:503
  80.2 1.2 %copy.12 = f32[4]{0:T(128)} copy(f32[4]{0:T(128)} %get-tuple-element.8) | data formatting | bytes 32
  81.4 1.9 %copy.13 = f32[8,2,8320]{2,1,0:T(2,128)} copy(f32[8,2,8320]{2,1,0:T(2,128)} %get-tuple-element.9) | data formatting | bytes 1064960

commit v9 on v8

--- a/solution.py
+++ b/solution.py
@@ -21,7 +21,6 @@
 SIZES = (5, 7, 8, 8, 5)
 STARTS = (0, 5, 12, 20, 28, 33)
 CHUNKS = len(SIZES)
-OTHERS = [(dz, dy) for dz in range(NZ) for dy in range(NY) if (dz, dy) != (0, 0)]
 F32 = jnp.float32
 BF16 = jnp.bfloat16
 HI = lax.Precision.HIGHEST
@@ -31,7 +30,7 @@
     img_ref, proj_ref, ctf_ref, noise_ref, trig_ref, shift_ref, class_ref,
     out_ref, ev_ref,
     placed, ometa, pair, pmeta, smeta, gath, praw, ctfh, weights, norms, normrows, onehot, ctfrows, vtab, prep,
-    score, pscore, stats, post, part, from_a, from_b, from_p, from_m, zsend, zrecv, keep, fin,
+    score, pscore, stats, zstats, post, part, from_a, from_b, from_p, from_m, zsend, zrecv, keep, fin,
     loc_sem, core_s, core_r, meta_s, meta_r, stat_s, stat_r, z_s, z_r,
     yp_s, ym_s, yl_r, yr_r, fa_s, fb_s, fa_r, fb_r, sc_s, sc_r,
     a_s, b_s, a_r, b_r, p_s, m_s, p_r, m_r, w_s, w_r, f_s, f_r,
@@ -54,13 +53,14 @@
         )
 
     peer = dev(core_=1 - core)
-    others = [dev(zl_=(zl + dz) % 4, y_=(y + dy) % 4) for dz, dy in OTHERS]
+    along_y = [dev(y_=(y + d) % 4) for d in (1, 2, 3)]
+    along_z = [dev(zl_=(zl + d) % 4) for d in (1, 2, 3)]
     right, left = dev(x_=xp), dev(x_=xm)
     up, down = dev(y_=yp), dev(y_=ym)
     across = [dev(zh_=1 - zh, core_=k) for k in range(2)]
 
     barrier = pltpu.get_barrier_semaphore()
-    greeted = [peer, *others, right, left, *across]
+    greeted = [peer, *along_y, *along_z, right, left, *across]
     for target in greeted:
         pl.semaphore_signal(barrier, inc=1, device_id=target, device_id_type=pl.DeviceIdType.MESH)
 
@@ -110,11 +110,16 @@
 
     pmeta_copy.wait_recv()
     smeta[own] = ometa[...] + pmeta[...]
-    meta_copies = [
+    meta_y = [
         send(smeta.at[own], smeta.at[own], meta_s.at[n], meta_r.at[n], target)
-        for n, target in enumerate(others)
-    ]
-    for copy in meta_copies:
+        for n, target in enumerate(along_y)
+    ]
+    column = pl.ds(zl * 4, 4)
+    meta_z = [
+        send(smeta.at[column], smeta.at[column], meta_s.at[3 + n], meta_r.at[3 + n], target)
+        for n, target in enumerate(along_z)
+    ]
+    for copy in meta_y:
         copy.start()
 
     pair_copy.wait_recv()
@@ -311,12 +316,16 @@
 
         lax.fori_loop(0, 3, three, 0)
 
+    for copy in meta_y:
+        copy.wait_recv()
+    for copy in meta_z:
+        copy.start()
     ctf_copy.wait()
     proj_copy.wait()
     praw_copy.wait_recv()
     half_norms = lax.fori_loop(0, 4, weigh, jnp.zeros((64, 128), F32))
 
-    for copy in meta_copies:
+    for copy in meta_z:
         copy.wait_recv()
 
     lane2 = lax.broadcasted_iota(jnp.int32, (8, 256), 1)
@@ -355,21 +364,30 @@
     summarise(2)
     summarise(3)
 
-    stat_copies = [
+    def merge(values):
+        peak = values[0][0:8]
+        for value in values[1:]:
+            peak = jnp.maximum(peak, value[0:8])
+        return peak, sum(value[8:16] * jnp.exp(value[0:8] - peak) for value in values)
+
+    stat_y = [
         send(stats.at[own], stats.at[own], stat_s.at[n], stat_r.at[n], target)
-        for n, target in enumerate(others)
-    ]
-    for copy in stat_copies:
+        for n, target in enumerate(along_y)
+    ]
+    for copy in stat_y:
         copy.start()
-    for copy in stat_copies:
+    for copy in stat_y:
         copy.wait_recv()
-    tops = [stats[b, 0:8, :] for b in range(BLOCKS)]
-    top = tops[0]
-    for b in range(1, BLOCKS):
-        top = jnp.maximum(top, tops[b])
-    total = jnp.zeros((8, LANES), F32)
-    for b in range(BLOCKS):
-        total += stats[b, 8:16, :] * jnp.exp(tops[b] - top)
+    zstats[zl] = jnp.concatenate(merge([stats[zl * 4 + k] for k in range(4)]), axis=0)
+    stat_z = [
+        send(zstats.at[zl], zstats.at[zl], stat_s.at[3 + n], stat_r.at[3 + n], target)
+        for n, target in enumerate(along_z)
+    ]
+    for copy in stat_z:
+        copy.start()
+    for copy in stat_z:
+        copy.wait_recv()
+    top, total = merge([zstats[k] for k in range(4)])
     held = lax.broadcasted_iota(jnp.int32, (8, LANES), 1) % 32
 
     def turn(value, by):
@@ -474,7 +492,7 @@
     pmeta_copy.wait_send()
     pair_copy.wait_send()
     praw_copy.wait_send()
-    for copy in meta_copies + stat_copies + sc_copies + y_up + y_down + fwd_up + fwd_down:
+    for copy in meta_y + meta_z + stat_y + stat_z + sc_copies + y_up + y_down + fwd_up + fwd_down:
         copy.wait_send()
     for q in range(4):
         pl.when(goes_right[q])(lambda q=q: z_right[q].wait_send())
@@ -498,7 +516,7 @@
     hbm = pl.BlockSpec(memory_space=pl.ANY)
     smem = pl.BlockSpec(memory_space=pltpu.SMEM)
     dma = pltpu.SemaphoreType.DMA
-    sems = [dma((2,)), dma((3,)), dma((3,)), dma((15,)), dma((15,)), dma((15,)), dma((15,))]
+    sems = [dma((2,)), dma((3,)), dma((3,)), dma((6,)), dma((6,)), dma((6,)), dma((6,))]
     sems += [dma((8,)), dma((4,))] + [dma((4,))] * 10 + [dma((CHUNKS,))] * 8 + [dma((CHUNKS, 2))] * 2 + [dma((CHUNKS,))] * 2
     sums, evidence = pl.pallas_call(
         kernel,
@@ -527,6 +545,7 @@
             pltpu.VMEM((4, 128, 128), F32),
             pltpu.VMEM((4, 128, 128), F32),
             pltpu.VMEM((BLOCKS, 16, LANES), F32),
+            pltpu.VMEM((NZ, 16, LANES), F32),
             pltpu.VMEM((128, 512), BF16),
             [pltpu.VMEM((8, 16, 256 * t), BF16) for t in SIZES],
             [pltpu.VMEM((16, 256 * t), BF16) for t in SIZES],

time: 83.5 us -> 84.9 us (1.017)
  Pallas kernels: 76.4 us -> 77.8 us
    pallas_call x1, Pallas kernels: 76.4 us -> 77.8 us  [per_device(): pl.pallas_call(kernel, out_shape=(jax.ShapeDtypeStruct((8, 2, pixels), F3...]
where the time goes in v9:
time: 84.9 us; the launch traced here: 84.7 us
  Pallas kernels  77.8 us (92%)
  local copies, waits for them, and re-layouts  6.22 us (7%)
    pallas_call x1, Pallas kernels, per_device(): pl.pallas_call(kernel, out_shape=(jax.ShapeDtypeStruct((8, 2, pixels), F3...  77.8 us
    transpose x1, local copies, waits for them, and re-layouts, per_device(): proj = projections.transpose(1, 0, 2).reshape(128, pixels)  3.16 us
    unnamed x2, local copies, waits for them, and re-layouts  3.06 us

profile of v9, /device:TPU:1, one launch (start us, length us, event | category | flops | bytes accessed | tf_op | source)
XLA Modules:
  0.0 84.7 jit_solution(12096617563502433687)
XLA Ops:
  0.6 3.2 %copy.9 = bf16[2,64,8320]{2,1,0:T(8,128)(2,1)} copy(bf16[2,64,8320]{2,0,1:T(2,128)(2,1)} %bitcast.5) | data formatting | bytes 4259840 | tf_op jit(solution)/shard_map/transpose | solution.py:511
  3.8 77.8 %shard_map.86 = (f32[8,2,8320]{2,1,0:T(2,128)}, f32[4]{0:T(128)}) custom-call(bf16[4,2,8320]{2,1,0:T(2,128)(2,1)} %img_ref.1, bf16[128,8320]{1,0:T(8,128)(2,1)} %bitcast.4, f32[64,8320]{1,0:T(8,128)} %ctf_ref.1, f32[65,128]{1,0:T(8,128)} %bitcast.6, f32[16,128]{1,0:T(8,128)} %constant.2.clone.trig_ref, s32[4,2,4]{2,1,0:T(2,128)} %bitcast.7, s32[4]{0:T(128)} %class_ref.1), custom_call_target="tpu_custom_call" | custom-call | tf_op jit(solution)/shard_map/pallas_call | solution.py:521
  81.6 1.2 %copy.12 = f32[4]{0:T(128)} copy(f32[4]{0:T(128)} %get-tuple-element.8) | data formatting | bytes 32
  82.8 1.9 %copy.13 = f32[8,2,8320]{2,1,0:T(2,128)} copy(f32[8,2,8320]{2,1,0:T(2,128)} %get-tuple-element.9) | data formatting | bytes 1064960

commit v10 on v8

--- a/solution.py
+++ b/solution.py
@@ -466,10 +466,16 @@
                         :, s * 256 + k * 128 : s * 256 + k * 128 + 128
                     ]
 
-    for n in range(CHUNKS + 4):
-        for lag, stage in ((0, project), (1, pass_on), (2, collect), (4, complete)):
-            if 0 <= n - lag < CHUNKS:
-                stage(n - lag)
+    for c in range(CHUNKS):
+        project(c)
+    for c in range(CHUNKS):
+        pass_on(c)
+    for c in range(CHUNKS):
+        collect(c)
+        if c >= 2:
+            complete(c - 2)
+    complete(CHUNKS - 2)
+    complete(CHUNKS - 1)
 
     pmeta_copy.wait_send()
     pair_copy.wait_send()

time: 83.5 us -> 82.7 us (level)
  no operation moved by 1% of the time
where the time goes in v10:
time: 82.7 us; the launch traced here: 82.5 us
  Pallas kernels  75.7 us (92%)
  local copies, waits for them, and re-layouts  6.22 us (8%)
    pallas_call x1, Pallas kernels, per_device(): pl.pallas_call(kernel, out_shape=(jax.ShapeDtypeStruct((8, 2, pixels), F3...  75.7 us
    transpose x1, local copies, waits for them, and re-layouts, per_device(): proj = projections.transpose(1, 0, 2).reshape(128, pixels)  3.16 us
    unnamed x2, local copies, waits for them, and re-layouts  3.06 us

profile of v10, /device:TPU:1, one launch (start us, length us, event | category | flops | bytes accessed | tf_op | source)
XLA Modules:
  0.0 82.5 jit_solution(6734346200778156773)
XLA Ops:
  0.6 3.2 %copy.9 = bf16[2,64,8320]{2,1,0:T(8,128)(2,1)} copy(bf16[2,64,8320]{2,0,1:T(2,128)(2,1)} %bitcast.5) | data formatting | bytes 4259840 | tf_op jit(solution)/shard_map/transpose | solution.py:499
  3.8 75.7 %shard_map.86 = (f32[8,2,8320]{2,1,0:T(2,128)}, f32[4]{0:T(128)}) custom-call(bf16[4,2,8320]{2,1,0:T(2,128)(2,1)} %img_ref.1, bf16[128,8320]{1,0:T(8,128)(2,1)} %bitcast.4, f32[64,8320]{1,0:T(8,128)} %ctf_ref.1, f32[65,128]{1,0:T(8,128)} %bitcast.6, f32[16,128]{1,0:T(8,128)} %constant.2.clone.trig_ref, s32[4,2,4]{2,1,0:T(2,128)} %bitcast.7, s32[4]{0:T(128)} %class_ref.1), custom_call_target="tpu_custom_call" | custom-call | tf_op jit(solution)/shard_map/pallas_call | solution.py:509
  79.5 1.2 %copy.12 = f32[4]{0:T(128)} copy(f32[4]{0:T(128)} %get-tuple-element.8) | data formatting | bytes 32
  80.7 1.9 %copy.13 = f32[8,2,8320]{2,1,0:T(2,128)} copy(f32[8,2,8320]{2,1,0:T(2,128)} %get-tuple-element.9) | data formatting | bytes 1064960

commit v11 on v10

--- a/solution.py
+++ b/solution.py
@@ -129,37 +129,36 @@
 
     order = [zl, pick([1, 0, 3, 2]), pick([2, 2, 1, 1]), pick([3, 3, 0, 0])]
 
-    def z_copy(zq, step, target):
-        b = zq * 4 + y
-        return send(gath.at[b], gath.at[b], z_s.at[step], z_r.at[zq], target)
-
-    z_right = [z_copy(order[q], q, dev(zl_=zl + 1)) for q in range(4)]
-    z_left = [z_copy(order[q], 4 + q, dev(zl_=zl - 1)) for q in range(4)]
+    halves = (pl.ds(0, HALF_A), pl.ds(HALF_A, HALF - HALF_A))
+
+    def same(b, h, ss, rs, target):
+        ref = gath.at[b, :, halves[h]]
+        return send(ref, ref, ss, rs, target)
+
+    above, below = dev(zl_=zl + 1), dev(zl_=zl - 1)
     goes_right = [zl < 3] + [jnp.logical_and(order[q] < zl, zl < 3) for q in (1, 2, 3)]
     goes_left = [zl > 0] + [jnp.logical_and(order[q] > zl, zl > 0) for q in (1, 2, 3)]
-    y_up = [
-        send(gath.at[order[q] * 4 + y], gath.at[order[q] * 4 + y], yp_s.at[q], yl_r.at[q], up)
-        for q in range(4)
-    ]
-    y_down = [
-        send(gath.at[order[q] * 4 + y], gath.at[order[q] * 4 + y], ym_s.at[q], yr_r.at[q], down)
-        for q in range(4)
-    ]
-    first, second = pl.ds(0, HALF_A), pl.ds(HALF_A, HALF - HALF_A)
-    fwd_up, fwd_down = [], []
+    z_right, z_left, y_up, y_down, fwd_up, fwd_down = [], [], [], [], [], []
     for q in range(4):
-        low = gath.at[order[q] * 4 + ym, :, first]
-        high = gath.at[order[q] * 4 + yp, :, second]
-        fwd_up.append(send(low, low, fa_s.at[q], fa_r.at[q], up))
-        fwd_down.append(send(high, high, fb_s.at[q], fb_r.at[q], down))
-
-    def launch(q):
-        pl.when(goes_right[q])(lambda: z_right[q].start())
-        pl.when(goes_left[q])(lambda: z_left[q].start())
-        y_up[q].start()
-        y_down[q].start()
-
-    launch(0)
+        for h in range(2):
+            n, came = 2 * q + h, z_r.at[order[q] * 2 + h]
+            b = order[q] * 4 + y
+            z_right.append(same(b, h, z_s.at[n], came, above))
+            z_left.append(same(b, h, z_s.at[8 + n], came, below))
+            y_up.append(same(b, h, yp_s.at[n], yl_r.at[n], up))
+            y_down.append(same(b, h, ym_s.at[n], yr_r.at[n], down))
+        fwd_up.append(same(order[q] * 4 + ym, 0, fa_s.at[q], fa_r.at[q], up))
+        fwd_down.append(same(order[q] * 4 + yp, 1, fb_s.at[q], fb_r.at[q], down))
+
+    def launch(q, h):
+        n = 2 * q + h
+        pl.when(goes_right[q])(lambda: z_right[n].start())
+        pl.when(goes_left[q])(lambda: z_left[n].start())
+        y_up[n].start()
+        y_down[n].start()
+
+    launch(0, 0)
+    launch(0, 1)
 
     def fill_rows(s, carry):
         p = (s + 32 * core) * LANES + lane
@@ -294,17 +293,22 @@
         prepare(order[q] * 4 + y2)
         sc_copies[q].start()
 
-    def arrive(q):
-        z_right[q].wait_recv()
-        launch(q)
-
-    def forward(q):
-        y_up[q].wait_recv()
-        fwd_up[q].start()
-        y_down[q].wait_recv()
-        fwd_down[q].start()
+    def arrive(q, h):
+        z_right[2 * q + h].wait_recv()
+        launch(q, h)
+
+    def forward(q, h):
+        if h == 0:
+            y_up[2 * q].wait_recv()
+            fwd_up[q].start()
+        else:
+            y_down[2 * q + 1].wait_recv()
+            fwd_down[q].start()
 
     def prepare_three(q):
+        y_up[2 * q + 1].wait_recv()
+        y_down[2 * q].wait_recv()
+
         def three(i, carry):
             prepare(order[q] * 4 + (y + 3 + i) % 4)
             return carry
@@ -315,6 +319,11 @@
     proj_copy.wait()
     praw_copy.wait_recv()
     half_norms = lax.fori_loop(0, 4, weigh, jnp.zeros((64, 128), F32))
+    arrive(1, 0)
+    forward(0, 0)
+    half_norms = lax.fori_loop(4, 6, weigh, half_norms)
+    arrive(1, 1)
+    forward(0, 1)
 
     for copy in meta_copies:
         copy.wait_recv()
@@ -330,27 +339,31 @@
     lax.fori_loop(0, BLOCKS, fill_onehot, 0)
     lax.fori_loop(0, 3, fill_ctf, 0)
 
-    arrive(1)
-    forward(0)
-    half_norms = lax.fori_loop(4, 11, weigh, half_norms)
+    arrive(2, 0)
+    half_norms = lax.fori_loop(6, 9, weigh, half_norms)
+    arrive(2, 1)
+    forward(1, 0)
+    half_norms = lax.fori_loop(9, 11, weigh, half_norms)
     norms[...] = 0.5 * half_norms
     normrows[...] = jnp.dot(
         onehot[:, 0:64], norms[...], precision=HI, preferred_element_type=F32
     )
-    arrive(2)
+    forward(1, 1)
     prepare_three(0)
-    forward(1)
-    arrive(3)
+    arrive(3, 0)
+    finish(0)
+    arrive(3, 1)
+    forward(2, 0)
     prepare_three(1)
-    forward(2)
-    finish(0)
-    prepare_three(2)
-    forward(3)
+    forward(2, 1)
+    forward(3, 0)
     finish(1)
     summarise(0)
-    prepare_three(3)
+    prepare_three(2)
+    forward(3, 1)
     finish(2)
     summarise(1)
+    prepare_three(3)
     finish(3)
     summarise(2)
     summarise(3)
@@ -482,9 +495,9 @@
     praw_copy.wait_send()
     for copy in meta_copies + stat_copies + sc_copies + y_up + y_down + fwd_up + fwd_down:
         copy.wait_send()
-    for q in range(4):
-        pl.when(goes_right[q])(lambda q=q: z_right[q].wait_send())
-        pl.when(goes_left[q])(lambda q=q: z_left[q].wait_send())
+    for n in range(8):
+        pl.when(goes_right[n // 2])(lambda n=n: z_right[n].wait_send())
+        pl.when(goes_left[n // 2])(lambda n=n: z_left[n].wait_send())
 
     for c in range(CHUNKS):
         for copy in (copy_a, copy_b, copy_p, copy_m, copy_f):
@@ -505,7 +518,7 @@
     smem = pl.BlockSpec(memory_space=pltpu.SMEM)
     dma = pltpu.SemaphoreType.DMA
     sems = [dma((2,)), dma((3,)), dma((3,)), dma((15,)), dma((15,)), dma((15,)), dma((15,))]
-    sems += [dma((8,)), dma((4,))] + [dma((4,))] * 10 + [dma((CHUNKS,))] * 8 + [dma((CHUNKS, 2))] * 2 + [dma((CHUNKS,))] * 2
+    sems += [dma((16,)), dma((8,))] + [dma((8,))] * 4 + [dma((4,))] * 6 + [dma((CHUNKS,))] * 8 + [dma((CHUNKS, 2))] * 2 + [dma((CHUNKS,))] * 2
     sums, evidence = pl.pallas_call(
         kernel,
         out_shape=(

time: 82.7 us -> 83.6 us (1.011)
  Pallas kernels: 75.7 us -> 76.6 us
    pallas_call x1, Pallas kernels: 75.7 us -> 76.6 us  [per_device(): pl.pallas_call(kernel, out_shape=(jax.ShapeDtypeStruct((8, 2, pixels), F3...]
where the time goes in v11:
time: 83.6 us; the launch traced here: 83.4 us
  Pallas kernels  76.6 us (92%)
  local copies, waits for them, and re-layouts  6.22 us (7%)
    pallas_call x1, Pallas kernels, per_device(): pl.pallas_call(kernel, out_shape=(jax.ShapeDtypeStruct((8, 2, pixels), F3...  76.6 us
    transpose x1, local copies, waits for them, and re-layouts, per_device(): proj = projections.transpose(1, 0, 2).reshape(128, pixels)  3.16 us
    unnamed x2, local copies, waits for them, and re-layouts  3.06 us

profile of v11, /device:TPU:1, one launch (start us, length us, event | category | flops | bytes accessed | tf_op | source)
XLA Modules:
  0.0 83.4 jit_solution(10650815467830817618)
XLA Ops:
  0.6 3.2 %copy.9 = bf16[2,64,8320]{2,1,0:T(8,128)(2,1)} copy(bf16[2,64,8320]{2,0,1:T(2,128)(2,1)} %bitcast.5) | data formatting | bytes 4259840 | tf_op jit(solution)/shard_map/transpose | solution.py:512
  3.8 76.6 %shard_map.86 = (f32[8,2,8320]{2,1,0:T(2,128)}, f32[4]{0:T(128)}) custom-call(bf16[4,2,8320]{2,1,0:T(2,128)(2,1)} %img_ref.1, bf16[128,8320]{1,0:T(8,128)(2,1)} %bitcast.4, f32[64,8320]{1,0:T(8,128)} %ctf_ref.1, f32[65,128]{1,0:T(8,128)} %bitcast.6, f32[16,128]{1,0:T(8,128)} %constant.2.clone.trig_ref, s32[4,2,4]{2,1,0:T(2,128)} %bitcast.7, s32[4]{0:T(128)} %class_ref.1), custom_call_target="tpu_custom_call" | custom-call | tf_op jit(solution)/shard_map/pallas_call | solution.py:522
  80.4 1.2 %copy.12 = f32[4]{0:T(128)} copy(f32[4]{0:T(128)} %get-tuple-element.8) | data formatting | bytes 32
  81.6 1.9 %copy.13 = f32[8,2,8320]{2,1,0:T(2,128)} copy(f32[8,2,8320]{2,1,0:T(2,128)} %get-tuple-element.9) | data formatting | bytes 1064960

commit v12 on v11

--- a/solution.py
+++ b/solution.py
@@ -28,13 +28,14 @@
 
 
 def kernel(
-    img_ref, proj_ref, ctf_ref, noise_ref, trig_ref, shift_ref, class_ref,
-    out_ref, ev_ref,
+    img_hbm, proj_ref, ctf_ref, noise_hbm, trig_hbm, shift_ref, class_ref,
+    out_hbm, ev_ref,
+    img_ref, noise_ref, trig_ref, out_ref,
     placed, ometa, pair, pmeta, smeta, gath, praw, ctfh, weights, norms, normrows, onehot, ctfrows, vtab, prep,
     score, pscore, stats, post, part, from_a, from_b, from_p, from_m, zsend, zrecv, keep, fin,
     loc_sem, core_s, core_r, meta_s, meta_r, stat_s, stat_r, z_s, z_r,
     yp_s, ym_s, yl_r, yr_r, fa_s, fb_s, fa_r, fb_r, sc_s, sc_r,
-    a_s, b_s, a_r, b_r, p_s, m_s, p_r, m_r, w_s, w_r, f_s, f_r,
+    a_s, b_s, a_r, b_r, p_s, m_s, p_r, m_r, w_s, w_r, f_s, f_r, out_sem,
 ):
     img = lax.axis_index("img")
     ori = lax.axis_index("ori")
@@ -59,6 +60,10 @@
     up, down = dev(y_=yp), dev(y_=ym)
     across = [dev(zh_=1 - zh, core_=k) for k in range(2)]
 
+    img_copy = pltpu.make_async_copy(img_hbm, img_ref, loc_sem.at[2])
+    noise_copy = pltpu.make_async_copy(noise_hbm, noise_ref, loc_sem.at[3])
+    trig_copy = pltpu.make_async_copy(trig_hbm, trig_ref, loc_sem.at[4])
+    img_copy.start()
     barrier = pltpu.get_barrier_semaphore()
     greeted = [peer, *others, right, left, *across]
     for target in greeted:
@@ -70,6 +75,8 @@
     proj_copy = pltpu.make_async_copy(proj_ref.at[:, mine], praw.at[core], loc_sem.at[1])
     ctf_copy.start()
     proj_copy.start()
+    noise_copy.start()
+    trig_copy.start()
 
     lane = lax.broadcasted_iota(jnp.int32, (8, LANES), 1)
     place = lax.broadcasted_iota(jnp.int32, (8, LANES), 0)
@@ -87,6 +94,7 @@
         placed[:, cols] = jnp.concatenate([real, imag], axis=0).astype(BF16)
         return carry
 
+    img_copy.wait()
     lax.fori_loop(0, 13, lay_out, 0)
     meta = jnp.zeros((8, LANES), jnp.int32)
     for i in range(4):
@@ -213,11 +221,10 @@
         weights[pl.ds(pl.multiple_of(n * 768, 768), 768), :] = jnp.concatenate(turned, axis=0)
         return total
 
-    cosine = trig_ref[0:8, :]
-    sine = trig_ref[8:16, :]
-
     def prepare(b):
         meta = smeta[b].astype(F32)[0:8, :].astype(jnp.int32)
+
+        cosine, sine = trig_ref[0:8, :], trig_ref[8:16, :]
 
         def wave(steps):
             index = steps & (KY - 1)
@@ -316,12 +323,14 @@
         lax.fori_loop(0, 3, three, 0)
 
     ctf_copy.wait()
+    noise_copy.wait()
+    trig_copy.wait()
     proj_copy.wait()
     praw_copy.wait_recv()
-    half_norms = lax.fori_loop(0, 4, weigh, jnp.zeros((64, 128), F32))
+    half_norms = lax.fori_loop(0, 4, weigh, jnp.zeros((64, 128), F32), unroll=4)
     arrive(1, 0)
     forward(0, 0)
-    half_norms = lax.fori_loop(4, 6, weigh, half_norms)
+    half_norms = lax.fori_loop(4, 6, weigh, half_norms, unroll=2)
     arrive(1, 1)
     forward(0, 1)
 
@@ -340,10 +349,10 @@
     lax.fori_loop(0, 3, fill_ctf, 0)
 
     arrive(2, 0)
-    half_norms = lax.fori_loop(6, 9, weigh, half_norms)
+    half_norms = lax.fori_loop(6, 9, weigh, half_norms, unroll=3)
     arrive(2, 1)
     forward(1, 0)
-    half_norms = lax.fori_loop(9, 11, weigh, half_norms)
+    half_norms = lax.fori_loop(9, 11, weigh, half_norms, unroll=2)
     norms[...] = 0.5 * half_norms
     normrows[...] = jnp.dot(
         onehot[:, 0:64], norms[...], precision=HI, preferred_element_type=F32
@@ -473,11 +482,24 @@
             rows = zrecv[c][half].astype(F32)
             value = near + jnp.concatenate([rows[0:8], rows[8:16]], axis=1)
             for s in range(SIZES[c]):
-                at = pl.multiple_of(half * SHIFT + (STARTS[c] + s) * LANES, LANES)
+                at = pl.ds((STARTS[c] + s) * LANES, LANES)
                 for k in range(2):
-                    out_ref[:, k, pl.ds(at, LANES)] = value[
-                        :, s * 256 + k * 128 : s * 256 + k * 128 + 128
-                    ]
+                    out_ref[half, :, k, at] = value[:, s * 256 + k * 128 : s * 256 + k * 128 + 128]
+            out_copy(c, half).start()
+
+    def out_copy(c, half):
+        skip = 1 if c == 0 else 0
+        count = (SIZES[c] - skip) * LANES
+        start = (STARTS[c] + skip) * LANES
+        return pltpu.make_async_copy(
+            out_ref.at[half, :, :, pl.ds(start, count)],
+            out_hbm.at[:, :, pl.ds(pl.multiple_of(half * SHIFT + start, LANES), count)],
+            out_sem.at[half, c],
+        )
+
+    first_tile = pltpu.make_async_copy(
+        out_ref.at[0, :, :, pl.ds(0, LANES)], out_hbm.at[:, :, pl.ds(0, LANES)], loc_sem.at[5]
+    )
 
     for c in range(CHUNKS):
         project(c)
@@ -487,8 +509,15 @@
         collect(c)
         if c >= 2:
             complete(c - 2)
+        if c == 2:
+            first_tile.start()
     complete(CHUNKS - 2)
     complete(CHUNKS - 1)
+
+    first_tile.wait()
+    for c in range(CHUNKS):
+        for half in range(2):
+            out_copy(c, half).wait()
 
     pmeta_copy.wait_send()
     pair_copy.wait_send()
@@ -513,21 +542,25 @@
     angles = np.arange(KY) * (2.0 * math.pi / KY)
     trig = np.concatenate([np.tile(np.cos(angles), (8, 1)), np.tile(np.sin(angles), (8, 1))])
     trig = jnp.asarray(trig.astype(np.float32))
-    vmem = pl.BlockSpec(memory_space=pltpu.VMEM)
     hbm = pl.BlockSpec(memory_space=pl.ANY)
     smem = pl.BlockSpec(memory_space=pltpu.SMEM)
     dma = pltpu.SemaphoreType.DMA
-    sems = [dma((2,)), dma((3,)), dma((3,)), dma((15,)), dma((15,)), dma((15,)), dma((15,))]
+    sems = [dma((6,)), dma((3,)), dma((3,)), dma((15,)), dma((15,)), dma((15,)), dma((15,))]
     sems += [dma((16,)), dma((8,))] + [dma((8,))] * 4 + [dma((4,))] * 6 + [dma((CHUNKS,))] * 8 + [dma((CHUNKS, 2))] * 2 + [dma((CHUNKS,))] * 2
+    sems += [dma((2, CHUNKS))]
     sums, evidence = pl.pallas_call(
         kernel,
         out_shape=(
             jax.ShapeDtypeStruct((8, 2, pixels), F32),
             jax.ShapeDtypeStruct((local,), F32),
         ),
-        in_specs=[vmem, hbm, hbm, vmem, vmem, smem, smem],
-        out_specs=(vmem, smem),
+        in_specs=[hbm, hbm, hbm, hbm, hbm, smem, smem],
+        out_specs=(hbm, smem),
         scratch_shapes=[
+            pltpu.VMEM((local, 2, pixels), BF16),
+            pltpu.VMEM((65, LANES), F32),
+            pltpu.VMEM((16, LANES), F32),
+            pltpu.VMEM((2, 8, 2, HALF), F32),
             pltpu.VMEM((16, 65 * LANES), BF16),
             pltpu.VMEM((16, LANES), BF16),
             pltpu.VMEM((16, HALF), BF16),

time: 83.6 us -> 83.8 us (level)
  no operation moved by 1% of the time
where the time goes in v12:
time: 83.8 us; the launch traced here: 83.6 us
  Pallas kernels  76.7 us (92%)
  local copies, waits for them, and re-layouts  6.22 us (7%)
    pallas_call x1, Pallas kernels, per_device(): pl.pallas_call(kernel, out_shape=(jax.ShapeDtypeStruct((8, 2, pixels), F3...  76.7 us
    transpose x1, local copies, waits for them, and re-layouts, per_device(): proj = projections.transpose(1, 0, 2).reshape(128, pixels)  3.16 us
    unnamed x2, local copies, waits for them, and re-layouts  3.06 us

profile of v12, /device:TPU:1, one launch (start us, length us, event | category | flops | bytes accessed | tf_op | source)
XLA Modules:
  0.0 83.6 jit_solution(6487511293109981689)
XLA Ops:
  0.6 3.2 %copy.9 = bf16[2,64,8320]{2,1,0:T(8,128)(2,1)} copy(bf16[2,64,8320]{2,0,1:T(2,128)(2,1)} %bitcast.5) | data formatting | bytes 4259840 | tf_op jit(solution)/shard_map/transpose | solution.py:541
  3.8 76.7 %shard_map.86 = (f32[8,2,8320]{2,1,0:T(2,128)}, f32[4]{0:T(128)}) custom-call(bf16[4,2,8320]{2,1,0:T(2,128)(2,1)} %img_hbm.1, bf16[128,8320]{1,0:T(8,128)(2,1)} %bitcast.4, f32[64,8320]{1,0:T(8,128)} %ctf_ref.1, f32[65,128]{1,0:T(8,128)} %bitcast.6, f32[16,128]{1,0:T(8,128)} %constant.2.clone.trig_hbm, s32[4,2,4]{2,1,0:T(2,128)} %bitcast.7, s32[4]{0:T(128)} %class_ref.1), custom_call_target="tpu_custom_call" | custom-call | tf_op jit(solution)/shard_map/pallas_call | solution.py:551
  80.5 1.2 %copy.12 = f32[4]{0:T(128)} copy(f32[4]{0:T(128)} %get-tuple-element.8) | data formatting | bytes 32
  81.7 1.9 %copy.13 = f32[8,2,8320]{2,1,0:T(2,128)} copy(f32[8,2,8320]{2,1,0:T(2,128)} %get-tuple-element.9) | data formatting | bytes 1064960

commit v13 on v12

--- a/solution.py
+++ b/solution.py
@@ -32,7 +32,7 @@
     out_hbm, ev_ref,
     img_ref, noise_ref, trig_ref, out_ref,
     placed, ometa, pair, pmeta, smeta, gath, praw, ctfh, weights, norms, normrows, onehot, ctfrows, vtab, prep,
-    score, pscore, stats, post, part, from_a, from_b, from_p, from_m, zsend, zrecv, keep, fin,
+    score, pscore, stats, post, part, from_a, from_b, from_p, from_m, zsend, zrecv, keep, fsend, fin,
     loc_sem, core_s, core_r, meta_s, meta_r, stat_s, stat_r, z_s, z_r,
     yp_s, ym_s, yl_r, yr_r, fa_s, fb_s, fa_r, fb_r, sc_s, sc_r,
     a_s, b_s, a_r, b_r, p_s, m_s, p_r, m_r, w_s, w_r, f_s, f_r, out_sem,
@@ -114,7 +114,6 @@
     praw_copy = send(proj_ref.at[:, theirs], praw.at[core], core_s.at[2], core_r.at[2], peer)
     pmeta_copy.start()
     pair_copy.start()
-    praw_copy.start()
 
     pmeta_copy.wait_recv()
     smeta[own] = ometa[...] + pmeta[...]
@@ -167,6 +166,7 @@
 
     launch(0, 0)
     launch(0, 1)
+    praw_copy.start()
 
     def fill_rows(s, carry):
         p = (s + 32 * core) * LANES + lane
@@ -323,31 +323,30 @@
         lax.fori_loop(0, 3, three, 0)
 
     ctf_copy.wait()
+    for copy in meta_copies:
+        copy.wait_recv()
+
+    lane2 = lax.broadcasted_iota(jnp.int32, (8, 256), 1)
+
+    def fill_onehot(b, carry):
+        classes = smeta[b].astype(F32)[0:8, 8:9].astype(jnp.int32)
+        hit = jnp.logical_and(lane2 % 64 == classes, lane2 < 192)
+        onehot[pl.ds(pl.multiple_of(b * 8, 8), 8), :] = hit.astype(F32)
+        return carry
+
+    lax.fori_loop(0, BLOCKS, fill_onehot, 0)
+    lax.fori_loop(0, 3, fill_ctf, 0)
+
+    arrive(1, 0)
+    forward(0, 0)
     noise_copy.wait()
     trig_copy.wait()
     proj_copy.wait()
     praw_copy.wait_recv()
     half_norms = lax.fori_loop(0, 4, weigh, jnp.zeros((64, 128), F32), unroll=4)
-    arrive(1, 0)
-    forward(0, 0)
-    half_norms = lax.fori_loop(4, 6, weigh, half_norms, unroll=2)
     arrive(1, 1)
     forward(0, 1)
-
-    for copy in meta_copies:
-        copy.wait_recv()
-
-    lane2 = lax.broadcasted_iota(jnp.int32, (8, 256), 1)
-
-    def fill_onehot(b, carry):
-        classes = smeta[b].astype(F32)[0:8, 8:9].astype(jnp.int32)
-        hit = jnp.logical_and(lane2 % 64 == classes, lane2 < 192)
-        onehot[pl.ds(pl.multiple_of(b * 8, 8), 8), :] = hit.astype(F32)
-        return carry
-
-    lax.fori_loop(0, BLOCKS, fill_onehot, 0)
-    lax.fori_loop(0, 3, fill_ctf, 0)
-
+    half_norms = lax.fori_loop(4, 6, weigh, half_norms, unroll=2)
     arrive(2, 0)
     half_norms = lax.fori_loop(6, 9, weigh, half_norms, unroll=3)
     arrive(2, 1)
@@ -434,8 +433,7 @@
         return send(zsend[c].at[0], zrecv[c].at[half], w_s.at[c, 0], w_r.at[c, half], across[0])
 
     def copy_f(c):
-        other = pl.ds(pl.multiple_of((1 - core) * 8, 8), 8)
-        return send(keep[c].at[other], fin[c], f_s.at[c], f_r.at[c], peer)
+        return send(fsend[c], fin[c], f_s.at[c], f_r.at[c], peer)
 
     def project(c):
         sums = jnp.dot(
@@ -470,7 +468,10 @@
             rows = away[8 * k : 8 * k + 8]
             zsend[c][k] = jnp.concatenate([rows[:, :half], rows[:, half:]], axis=0).astype(BF16)
             copy_w(c, k).start()
-        keep[c][...] = add(part[c][2 * x + zh], from_p[c][zh], from_m[c][zh])
+        near = add(part[c][2 * x + zh], from_p[c][zh], from_m[c][zh])
+        keep[c][...] = near
+        rows = jnp.where(core == 0, near[8:16], near[0:8])
+        fsend[c][...] = jnp.concatenate([rows[:, :half], rows[:, half:]], axis=0).astype(BF16)
         copy_f(c).start()
 
     def complete(c):
@@ -478,9 +479,12 @@
             arrived_w(c, half).wait_recv()
         copy_f(c).wait_recv()
         here = keep[c][pl.ds(pl.multiple_of(core * 8, 8), 8), :]
-        for half, near in ((core, here), (1 - core, fin[c][...])):
-            rows = zrecv[c][half].astype(F32)
-            value = near + jnp.concatenate([rows[0:8], rows[8:16]], axis=1)
+        def unfold(rows):
+            rows = rows.astype(F32)
+            return jnp.concatenate([rows[0:8], rows[8:16]], axis=1)
+
+        for half, near in ((core, here), (1 - core, unfold(fin[c][...]))):
+            value = near + unfold(zrecv[c][half])
             for s in range(SIZES[c]):
                 at = pl.ds((STARTS[c] + s) * LANES, LANES)
                 for k in range(2):
@@ -588,7 +592,8 @@
             [pltpu.VMEM((2, 16, 128 * t), BF16) for t in SIZES],
             [pltpu.VMEM((2, 16, 128 * t), BF16) for t in SIZES],
             [pltpu.VMEM((16, 256 * t), F32) for t in SIZES],
-            [pltpu.VMEM((8, 256 * t), F32) for t in SIZES],
+            [pltpu.VMEM((16, 128 * t), BF16) for t in SIZES],
+            [pltpu.VMEM((16, 128 * t), BF16) for t in SIZES],
             *sems,
         ],
         compiler_params=pltpu.CompilerParams(

time: 83.8 us -> 83.9 us (level)
  no operation moved by 1% of the time
where the time goes in v13:
time: 83.9 us; the launch traced here: 83.7 us
  Pallas kernels  76.8 us (92%)
  local copies, waits for them, and re-layouts  6.22 us (7%)
    pallas_call x1, Pallas kernels, per_device(): pl.pallas_call(kernel, out_shape=(jax.ShapeDtypeStruct((8, 2, pixels), F3...  76.8 us
    transpose x1, local copies, waits for them, and re-layouts, per_device(): proj = projections.transpose(1, 0, 2).reshape(128, pixels)  3.16 us
    unnamed x2, local copies, waits for them, and re-layouts  3.06 us

profile of v13, /device:TPU:1, one launch (start us, length us, event | category | flops | bytes accessed | tf_op | source)
XLA Modules:
  0.0 83.7 jit_solution(1954861679591153791)
XLA Ops:
  0.6 3.2 %copy.9 = bf16[2,64,8320]{2,1,0:T(8,128)(2,1)} copy(bf16[2,64,8320]{2,0,1:T(2,128)(2,1)} %bitcast.5) | data formatting | bytes 4259840 | tf_op jit(solution)/shard_map/transpose | solution.py:545
  3.8 76.8 %shard_map.86 = (f32[8,2,8320]{2,1,0:T(2,128)}, f32[4]{0:T(128)}) custom-call(bf16[4,2,8320]{2,1,0:T(2,128)(2,1)} %img_hbm.1, bf16[128,8320]{1,0:T(8,128)(2,1)} %bitcast.4, f32[64,8320]{1,0:T(8,128)} %ctf_ref.1, f32[65,128]{1,0:T(8,128)} %bitcast.6, f32[16,128]{1,0:T(8,128)} %constant.2.clone.trig_hbm, s32[4,2,4]{2,1,0:T(2,128)} %bitcast.7, s32[4]{0:T(128)} %class_ref.1), custom_call_target="tpu_custom_call" | custom-call | tf_op jit(solution)/shard_map/pallas_call | solution.py:555
  80.6 1.2 %copy.12 = f32[4]{0:T(128)} copy(f32[4]{0:T(128)} %get-tuple-element.8) | data formatting | bytes 32
  81.8 1.9 %copy.13 = f32[8,2,8320]{2,1,0:T(2,128)} copy(f32[8,2,8320]{2,1,0:T(2,128)} %get-tuple-element.9) | data formatting | bytes 1064960

commit v14 on v11

--- a/solution.py
+++ b/solution.py
@@ -213,11 +213,8 @@
         weights[pl.ds(pl.multiple_of(n * 768, 768), 768), :] = jnp.concatenate(turned, axis=0)
         return total
 
-    cosine = trig_ref[0:8, :]
-    sine = trig_ref[8:16, :]
-
-    def prepare(b):
-        meta = smeta[b].astype(F32)[0:8, :].astype(jnp.int32)
+    def prepare(*bs):
+        cosine, sine = trig_ref[0:8, :], trig_ref[8:16, :]
 
         def wave(steps):
             index = steps & (KY - 1)
@@ -227,49 +224,68 @@
             )
 
         begin, one_row, two_rows = [], [], []
-        for t in range(TRANS):
-            sx = meta[:, 2 * t : 2 * t + 1]
-            sy = meta[:, 2 * t + 1 : 2 * t + 2]
-            slope = jnp.broadcast_to(sy - KX * sx, (8, LANES))
-            begin.append(wave(lane * sx + top_row * slope))
-            one_row.append(wave(slope))
-            two_rows.append(wave(2 * slope))
+        for b in bs:
+            meta = smeta[b].astype(F32)[0:8, :].astype(jnp.int32)
+            first_, one, two = [], [], []
+            for t in range(TRANS):
+                sx = meta[:, 2 * t : 2 * t + 1]
+                sy = meta[:, 2 * t + 1 : 2 * t + 2]
+                slope = jnp.broadcast_to(sy - KX * sx, (8, LANES))
+                first_.append(wave(lane * sx + top_row * slope))
+                one.append(wave(slope))
+                two.append(wave(2 * slope))
+            begin.append(tuple(first_))
+            one_row.append(one)
+            two_rows.append(two)
 
         def body(n, carry):
-            phases, total = carry
+            every, total = carry
             wide = pl.ds(pl.multiple_of(n * 384, 384), 384)
-            blocks = gath[b, :, wide].astype(F32)
-            ctfs = ctfrows[pl.ds(pl.multiple_of(b * 8, 8), 8), wide]
+            steps = pl.ds(pl.multiple_of(n * 768, 768), 768)
             singles = [vtab[3 * n + i] == 1 for i in range(3)]
-            rows = [[], []]
-            for i in range(3):
-                tile = slice(i * LANES, (i + 1) * LANES)
-                ctf = ctfs[:, tile]
-                real, imag = blocks[0:8, tile] * ctf, blocks[8:16, tile] * ctf
-                reals, imags, later = [], [], []
-                for t in range(TRANS):
-                    c, si = phases[t]
-                    reals.append(real * c + imag * si)
-                    imags.append(imag * c - real * si)
-                    mc = jnp.where(singles[i], one_row[t][0], two_rows[t][0])
-                    ms = jnp.where(singles[i], one_row[t][1], two_rows[t][1])
-                    later.append((c * mc - si * ms, si * mc + c * ms))
-                phases = tuple(later)
-                for h in range(2):
-                    for values in (reals, imags):
-                        pair_ = jnp.concatenate(values[2 * h : 2 * h + 2], axis=0)
-                        rows[h].append(pair_.astype(BF16))
-            steps = pl.ds(pl.multiple_of(n * 768, 768), 768)
-            made = jnp.concatenate([jnp.concatenate(r, axis=1) for r in rows], axis=0)
-            total = total + jnp.dot(made, weights[steps, :], preferred_element_type=F32)
-            prep[pl.ds(pl.multiple_of(b * 32, 32), 32), steps] = made
-            return phases, total
-
-        start = (tuple(begin), jnp.zeros((32, LANES), F32))
+            loaded = [
+                (gath[b, :, wide].astype(F32), ctfrows[pl.ds(pl.multiple_of(b * 8, 8), 8), wide])
+                for b in bs
+            ]
+            after, made = [], []
+            for k, phases in enumerate(every):
+                blocks, ctfs = loaded[k]
+                rows = [[], []]
+                for i in range(3):
+                    tile = slice(i * LANES, (i + 1) * LANES)
+                    ctf = ctfs[:, tile]
+                    real, imag = blocks[0:8, tile] * ctf, blocks[8:16, tile] * ctf
+                    reals, imags, later = [], [], []
+                    for t in range(TRANS):
+                        c, si = phases[t]
+                        reals.append(real * c + imag * si)
+                        imags.append(imag * c - real * si)
+                        mc = jnp.where(singles[i], one_row[k][t][0], two_rows[k][t][0])
+                        ms = jnp.where(singles[i], one_row[k][t][1], two_rows[k][t][1])
+                        later.append((c * mc - si * ms, si * mc + c * ms))
+                    phases = tuple(later)
+                    for h in range(2):
+                        for values in (reals, imags):
+                            pair_ = jnp.concatenate(values[2 * h : 2 * h + 2], axis=0)
+                            rows[h].append(pair_.astype(BF16))
+                after.append(phases)
+                made += [jnp.concatenate(r, axis=1) for r in rows]
+            for k, b in enumerate(bs):
+                at = pl.ds(pl.multiple_of(b * 32, 32), 32)
+                prep[at, steps] = jnp.concatenate(made[2 * k : 2 * k + 2], axis=0)
+            total = total + jnp.dot(
+                jnp.concatenate(made, axis=0), weights[steps, :], preferred_element_type=F32
+            )
+            return tuple(after), total
+
+        start = (tuple(begin), jnp.zeros((32 * len(bs), LANES), F32))
         _, cross = lax.fori_loop(0, TILES // 3, body, start, unroll=11)
-        norm = normrows[pl.ds(pl.multiple_of(b * 8, 8), 8), :]
-        at = pl.ds(pl.multiple_of((b % 4) * 32, 32), 32)
-        score[b // 4, at, :] = cross - jnp.concatenate([norm] * TRANS, axis=0)
+        for k, b in enumerate(bs):
+            norm = normrows[pl.ds(pl.multiple_of(b * 8, 8), 8), :]
+            at = pl.ds(pl.multiple_of((b % 4) * 32, 32), 32)
+            score[b // 4, at, :] = cross[32 * k : 32 * k + 32] - jnp.concatenate(
+                [norm] * TRANS, axis=0
+            )
 
     sc_copies = [
         send(score.at[order[q]], pscore.at[order[q]], sc_s.at[q], sc_r.at[q], peer)
@@ -287,11 +303,15 @@
         stats[own, pl.ds(g, 1), :] = top
         stats[own, pl.ds(8 + g, 1), :] = jnp.sum(jnp.exp(whole - top), axis=0, keepdims=True)
 
-    def finish(q):
+    def sides(q):
+        y_up[2 * q + 1].wait_recv()
+        y_down[2 * q].wait_recv()
+        prepare(order[q] * 4 + ym, order[q] * 4 + yp)
+
+    def farthest(q):
         fwd_up[q].wait_recv()
         fwd_down[q].wait_recv()
-        prepare(order[q] * 4 + y2)
-        sc_copies[q].start()
+        return order[q] * 4 + y2
 
     def arrive(q, h):
         z_right[2 * q + h].wait_recv()
@@ -304,16 +324,6 @@
         else:
             y_down[2 * q + 1].wait_recv()
             fwd_down[q].start()
-
-    def prepare_three(q):
-        y_up[2 * q + 1].wait_recv()
-        y_down[2 * q].wait_recv()
-
-        def three(i, carry):
-            prepare(order[q] * 4 + (y + 3 + i) % 4)
-            return carry
-
-        lax.fori_loop(0, 3, three, 0)
 
     ctf_copy.wait()
     proj_copy.wait()
@@ -349,22 +359,26 @@
         onehot[:, 0:64], norms[...], precision=HI, preferred_element_type=F32
     )
     forward(1, 1)
-    prepare_three(0)
+    prepare(order[0] * 4 + y, order[1] * 4 + y)
     arrive(3, 0)
-    finish(0)
+    sides(0)
     arrive(3, 1)
     forward(2, 0)
-    prepare_three(1)
+    sides(1)
     forward(2, 1)
+    prepare(farthest(0), order[2] * 4 + y)
+    sc_copies[0].start()
     forward(3, 0)
-    finish(1)
+    sides(2)
+    forward(3, 1)
+    prepare(farthest(1), order[3] * 4 + y)
+    sc_copies[1].start()
     summarise(0)
-    prepare_three(2)
-    forward(3, 1)
-    finish(2)
+    sides(3)
     summarise(1)
-    prepare_three(3)
-    finish(3)
+    prepare(farthest(2), farthest(3))
+    sc_copies[2].start()
+    sc_copies[3].start()
     summarise(2)
     summarise(3)
 
@@ -559,7 +573,7 @@
             *sems,
         ],
         compiler_params=pltpu.CompilerParams(
-            collective_id=0, has_side_effects=True, vmem_limit_bytes=56 * 1024 * 1024
+            collective_id=0, has_side_effects=True, vmem_limit_bytes=34 * 1024 * 1024
         ),
     )(
         images, proj, ctf_table, noise_weight.reshape(65, LANES), trig,

time: 83.6 us -> 78 us (0.933)
  Pallas kernels: 76.6 us -> 73.6 us
  local copies, waits for them, and re-layouts: 6.22 us -> 3.51 us
    pallas_call x1, Pallas kernels: 76.6 us -> 73.6 us  [per_device(): pl.pallas_call(kernel, out_shape=(jax.ShapeDtypeStruct((8, 2, pixels), F3...]
    unnamed x2 -> x14, local copies, waits for them, and re-layouts: 3.06 us -> 1.55 us
    transpose x1, local copies, waits for them, and re-layouts: 3.16 us -> 1.96 us  [per_device(): proj = projections.transpose(1, 0, 2).reshape(128, pixels)]
where the time goes in v14:
time: 78 us; the launch traced here: 77.8 us
  Pallas kernels  73.6 us (94%)
  local copies, waits for them, and re-layouts  3.51 us (4%)
    pallas_call x1, Pallas kernels, per_device(): pl.pallas_call(kernel, out_shape=(jax.ShapeDtypeStruct((8, 2, pixels), F3...  73.6 us
    transpose x1, local copies, waits for them, and re-layouts, per_device(): proj = projections.transpose(1, 0, 2).reshape(128, pixels)  1.96 us

profile of v14, /device:TPU:1, one launch (start us, length us, event | category | flops | bytes accessed | tf_op | source)
XLA Modules:
  0.0 77.8 jit_solution(3746343302351808127)
XLA Ops:
  0.6 0.0 copy-start
  0.6 0.0 copy-start.1
  0.7 0.0 copy-start.2
  0.7 0.0 copy-start.3
  0.7 0.0 copy-start.4
  0.7 0.0 copy-start.5
  0.7 2.0 %copy.9 = bf16[2,64,8320]{2,1,0:T(8,128)(2,1)S(1)} copy(bf16[2,64,8320]{2,0,1:T(2,128)(2,1)} %bitcast.7) | data formatting | bytes 4259840 | tf_op jit(solution)/shard_map/transpose | solution.py:526
  2.7 0.2 copy-done
  2.9 0.0 copy-done.1
  2.9 0.0 copy-done.2
  2.9 0.0 copy-done.3
  2.9 0.0 copy-done.4
  2.9 0.0 copy-done.5
  2.9 73.6 %shard_map.86 = (f32[8,2,8320]{2,1,0:T(2,128)S(1)}, f32[4]{0:T(128)S(1)}) custom-call(bf16[4,2,8320]{2,1,0:T(2,128)(2,1)S(1)} %copy-done.1, bf16[128,8320]{1,0:T(8,128)(2,1)S(1)} %bitcast.4, f32[64,8320]{1,0:T(8,128)S(1)} %copy-done, f32[65,128]{1,0:T(8,128)S(1)} %bitcast.5, f32[16,128]{1,0:T(8,128)S(1)} %copy-done.3, s32[4,2,4]{2,1,0:T(2,128)S(1)} %bitcast.6, ...), custom_call_target="tpu_custom_call" | custom-call | tf_op jit(solution)/shard_map/pallas_call | solution.py:536
  76.5 0.5 copy.12
  77.0 0.8 %copy.13 = f32[8,2,8320]{2,1,0:T(2,128)} copy(f32[8,2,8320]{2,1,0:T(2,128)S(1)} %get-tuple-element.9) | data formatting | bytes 1064960
Async XLA Ops:
  0.6 2.2 %copy-start = (f32[64,8320]{1,0:T(8,128)S(1)}, f32[64,8320]{1,0:T(8,128)}, u32[]{:S(2)}) copy-start(f32[64,8320]{1,0:T(8,128)} %ctf_ref.1) | copy-start | bytes 6389764
  0.6 2.2 %copy-start.1 = (bf16[4,2,8320]{2,1,0:T(2,128)(2,1)S(1)}, bf16[4,2,8320]{2,1,0:T(2,128)(2,1)}, u32[]{:S(2)}) copy-start(bf16[4,2,8320]{2,1,0:T(2,128)(2,1)} %img_ref.1) | copy-start | bytes 399364
  0.7 2.2 %copy-start.2 = (f32[8320]{0:T(1024)S(1)}, f32[8320]{0:T(1024)}, u32[]{:S(2)}) copy-start(f32[8320]{0:T(1024)} %param.10) | copy-start | bytes 99844
  0.7 2.2 %copy-start.3 = (f32[16,128]{1,0:T(8,128)S(1)}, f32[16,128]{1,0:T(8,128)}, u32[]{:S(2)}) copy-start(f32[16,128]{1,0:T(8,128)} %constant.2.clone.trig_ref) | copy-start | bytes 24580
  0.7 2.2 %copy-start.4 = (s32[4,4,2]{1,2,0:T(2,128)S(1)}, s32[4,4,2]{1,2,0:T(2,128)}, u32[]{:S(2)}) copy-start(s32[4,4,2]{1,2,0:T(2,128)} %param.11) | copy-start | bytes 388
  0.7 2.2 %copy-start.5 = (s32[4]{0:T(128)S(1)}, s32[4]{0:T(128)}, u32[]{:S(2)}) copy-start(s32[4]{0:T(128)} %class_ref.1) | copy-start | bytes 52

commit v15 on v14

--- a/solution.py
+++ b/solution.py
@@ -24,13 +24,12 @@
 OTHERS = [(dz, dy) for dz in range(NZ) for dy in range(NY) if (dz, dy) != (0, 0)]
 F32 = jnp.float32
 BF16 = jnp.bfloat16
-HI = lax.Precision.HIGHEST
 
 
 def kernel(
     img_ref, proj_ref, ctf_ref, noise_ref, trig_ref, shift_ref, class_ref,
     out_ref, ev_ref,
-    placed, ometa, pair, pmeta, smeta, gath, praw, ctfh, weights, norms, normrows, onehot, ctfrows, vtab, prep,
+    placed, ometa, pair, pmeta, smeta, gath, praw, ctfh, weights, normrows, onehot, ctfrows, vtab, prep,
     score, pscore, stats, post, part, from_a, from_b, from_p, from_m, zsend, zrecv, keep, fin,
     loc_sem, core_s, core_r, meta_s, meta_r, stat_s, stat_r, z_s, z_r,
     yp_s, ym_s, yl_r, yr_r, fa_s, fb_s, fa_r, fb_r, sc_s, sc_r,
@@ -328,10 +327,10 @@
     ctf_copy.wait()
     proj_copy.wait()
     praw_copy.wait_recv()
-    half_norms = lax.fori_loop(0, 4, weigh, jnp.zeros((64, 128), F32))
+    half_norms = lax.fori_loop(0, 4, weigh, jnp.zeros((64, 128), F32), unroll=4)
     arrive(1, 0)
     forward(0, 0)
-    half_norms = lax.fori_loop(4, 6, weigh, half_norms)
+    half_norms = lax.fori_loop(4, 6, weigh, half_norms, unroll=2)
     arrive(1, 1)
     forward(0, 1)
 
@@ -350,13 +349,15 @@
     lax.fori_loop(0, 3, fill_ctf, 0)
 
     arrive(2, 0)
-    half_norms = lax.fori_loop(6, 9, weigh, half_norms)
+    half_norms = lax.fori_loop(6, 9, weigh, half_norms, unroll=3)
     arrive(2, 1)
     forward(1, 0)
-    half_norms = lax.fori_loop(9, 11, weigh, half_norms)
-    norms[...] = 0.5 * half_norms
+    half_norms = lax.fori_loop(9, 11, weigh, half_norms, unroll=2)
+    one, two, three = pieces(0.5 * half_norms)
     normrows[...] = jnp.dot(
-        onehot[:, 0:64], norms[...], precision=HI, preferred_element_type=F32
+        onehot[...].astype(BF16),
+        jnp.concatenate([one, two, three, one], axis=0),
+        preferred_element_type=F32,
     )
     forward(1, 1)
     prepare(order[0] * 4 + y, order[1] * 4 + y)
@@ -551,7 +552,6 @@
             pltpu.VMEM((2, 128, HALF), BF16),
             pltpu.VMEM((64, HALF), F32),
             pltpu.VMEM((2 * HALF, 128), BF16),
-            pltpu.VMEM((64, 128), F32),
             pltpu.VMEM((128, 128), F32),
             pltpu.VMEM((128, 2 * LANES), F32),
             pltpu.VMEM((128, HALF), F32),

time: 78 us -> 78.4 us (level)
  no operation moved by 1% of the time
where the time goes in v15:
time: 78.4 us; the launch traced here: 78.1 us
  Pallas kernels  73.9 us (94%)
  local copies, waits for them, and re-layouts  3.51 us (4%)
    pallas_call x1, Pallas kernels, per_device(): pl.pallas_call(kernel, out_shape=(jax.ShapeDtypeStruct((8, 2, pixels), F3...  73.9 us
    transpose x1, local copies, waits for them, and re-layouts, per_device(): proj = projections.transpose(1, 0, 2).reshape(128, pixels)  1.96 us

profile of v15, /device:TPU:1, one launch (start us, length us, event | category | flops | bytes accessed | tf_op | source)
XLA Modules:
  0.0 78.1 jit_solution(381607077975866183)
XLA Ops:
  0.6 0.0 copy-start
  0.6 0.0 copy-start.1
  0.7 0.0 copy-start.2
  0.7 0.0 copy-start.3
  0.7 0.0 copy-start.4
  0.7 0.0 copy-start.5
  0.7 2.0 %copy.9 = bf16[2,64,8320]{2,1,0:T(8,128)(2,1)S(1)} copy(bf16[2,64,8320]{2,0,1:T(2,128)(2,1)} %bitcast.7) | data formatting | bytes 4259840 | tf_op jit(solution)/shard_map/transpose | solution.py:527
  2.7 0.2 copy-done
  2.9 0.0 copy-done.1
  2.9 0.0 copy-done.2
  2.9 0.0 copy-done.3
  2.9 0.0 copy-done.4
  2.9 0.0 copy-done.5
  2.9 73.9 %shard_map.86 = (f32[8,2,8320]{2,1,0:T(2,128)S(1)}, f32[4]{0:T(128)S(1)}) custom-call(bf16[4,2,8320]{2,1,0:T(2,128)(2,1)S(1)} %copy-done.1, bf16[128,8320]{1,0:T(8,128)(2,1)S(1)} %bitcast.4, f32[64,8320]{1,0:T(8,128)S(1)} %copy-done, f32[65,128]{1,0:T(8,128)S(1)} %bitcast.5, f32[16,128]{1,0:T(8,128)S(1)} %copy-done.3, s32[4,2,4]{2,1,0:T(2,128)S(1)} %bitcast.6, ...), custom_call_target="tpu_custom_call" | custom-call | tf_op jit(solution)/shard_map/pallas_call | solution.py:537
  76.8 0.5 copy.12
  77.4 0.8 %copy.13 = f32[8,2,8320]{2,1,0:T(2,128)} copy(f32[8,2,8320]{2,1,0:T(2,128)S(1)} %get-tuple-element.9) | data formatting | bytes 1064960
Async XLA Ops:
  0.6 2.2 %copy-start = (f32[64,8320]{1,0:T(8,128)S(1)}, f32[64,8320]{1,0:T(8,128)}, u32[]{:S(2)}) copy-start(f32[64,8320]{1,0:T(8,128)} %ctf_ref.1) | copy-start | bytes 6389764
  0.6 2.2 %copy-start.1 = (bf16[4,2,8320]{2,1,0:T(2,128)(2,1)S(1)}, bf16[4,2,8320]{2,1,0:T(2,128)(2,1)}, u32[]{:S(2)}) copy-start(bf16[4,2,8320]{2,1,0:T(2,128)(2,1)} %img_ref.1) | copy-start | bytes 399364
  0.7 2.2 %copy-start.2 = (f32[8320]{0:T(1024)S(1)}, f32[8320]{0:T(1024)}, u32[]{:S(2)}) copy-start(f32[8320]{0:T(1024)} %param.10) | copy-start | bytes 99844
  0.7 2.2 %copy-start.3 = (f32[16,128]{1,0:T(8,128)S(1)}, f32[16,128]{1,0:T(8,128)}, u32[]{:S(2)}) copy-start(f32[16,128]{1,0:T(8,128)} %constant.2.clone.trig_ref) | copy-start | bytes 24580
  0.7 2.2 %copy-start.4 = (s32[4,4,2]{1,2,0:T(2,128)S(1)}, s32[4,4,2]{1,2,0:T(2,128)}, u32[]{:S(2)}) copy-start(s32[4,4,2]{1,2,0:T(2,128)} %param.11) | copy-start | bytes 388
  0.7 2.2 %copy-start.5 = (s32[4]{0:T(128)S(1)}, s32[4]{0:T(128)}, u32[]{:S(2)}) copy-start(s32[4]{0:T(128)} %class_ref.1) | copy-start | bytes 52

commit v16 on v14

--- a/solution.py
+++ b/solution.py
@@ -30,9 +30,9 @@
 def kernel(
     img_ref, proj_ref, ctf_ref, noise_ref, trig_ref, shift_ref, class_ref,
     out_ref, ev_ref,
-    placed, ometa, pair, pmeta, smeta, gath, praw, ctfh, weights, norms, normrows, onehot, ctfrows, vtab, prep,
+    placed, ometa, pair, pmeta, smeta, gath, praw, weights, norms, normrows, onehot, ctfrows, vtab, prep,
     score, pscore, stats, post, part, from_a, from_b, from_p, from_m, zsend, zrecv, keep, fin,
-    loc_sem, core_s, core_r, meta_s, meta_r, stat_s, stat_r, z_s, z_r,
+    core_s, core_r, meta_s, meta_r, stat_s, stat_r, z_s, z_r,
     yp_s, ym_s, yl_r, yr_r, fa_s, fb_s, fa_r, fb_r, sc_s, sc_r,
     a_s, b_s, a_r, b_r, p_s, m_s, p_r, m_r, w_s, w_r, f_s, f_r,
 ):
@@ -66,10 +66,6 @@
 
     mine = pl.ds(pl.multiple_of(core * SHIFT, LANES), HALF)
     theirs = pl.ds(pl.multiple_of((1 - core) * SHIFT, LANES), HALF)
-    ctf_copy = pltpu.make_async_copy(ctf_ref.at[:, mine], ctfh, loc_sem.at[0])
-    proj_copy = pltpu.make_async_copy(proj_ref.at[:, mine], praw.at[core], loc_sem.at[1])
-    ctf_copy.start()
-    proj_copy.start()
 
     lane = lax.broadcasted_iota(jnp.int32, (8, LANES), 1)
     place = lax.broadcasted_iota(jnp.int32, (8, LANES), 0)
@@ -103,7 +99,7 @@
 
     pair_copy = send(placed.at[:, theirs], pair, core_s.at[0], core_r.at[0], peer)
     pmeta_copy = send(ometa, pmeta, core_s.at[1], core_r.at[1], peer)
-    praw_copy = send(proj_ref.at[:, theirs], praw.at[core], core_s.at[2], core_r.at[2], peer)
+    praw_copy = send(proj_ref.at[:, theirs], praw, core_s.at[2], core_r.at[2], peer)
     pmeta_copy.start()
     pair_copy.start()
     praw_copy.start()
@@ -178,7 +174,8 @@
 
     def fill_ctf(s, carry):
         cols = pl.ds(pl.multiple_of(s * 1408, 1408), 1408)
-        one, two, three = pieces(ctfh[:, cols])
+        there = pl.ds(pl.multiple_of(core * SHIFT + s * 1408, LANES), 1408)
+        one, two, three = pieces(ctf_ref[:, there])
         ctfrows[:, cols] = jnp.dot(
             onehot[...].astype(BF16),
             jnp.concatenate([one, two, three, one], axis=0),
@@ -189,8 +186,10 @@
 
     def weigh(n, total):
         wide = pl.ds(pl.multiple_of(n * 384, 384), 384)
-        raw = [praw[0, :, wide], praw[1, :, wide]]
-        ctfs = ctfh[:, wide]
+        there = pl.ds(pl.multiple_of(core * SHIFT + n * 384, LANES), 384)
+        here, far = proj_ref[:, there], praw[:, wide]
+        raw = [jnp.where(core == 0, here, far), jnp.where(core == 0, far, here)]
+        ctfs = ctf_ref[:, there]
         noises = [noise_ref[pl.ds(core * 32 + 3 * n + i, 1), :] for i in range(3)]
         counted = 1 - core * (1 - jnp.minimum(n, 1))
         noises[0] = noises[0] * counted.astype(F32)
@@ -325,8 +324,6 @@
             y_down[2 * q + 1].wait_recv()
             fwd_down[q].start()
 
-    ctf_copy.wait()
-    proj_copy.wait()
     praw_copy.wait_recv()
     half_norms = lax.fori_loop(0, 4, weigh, jnp.zeros((64, 128), F32))
     arrive(1, 0)
@@ -528,10 +525,9 @@
     trig = np.concatenate([np.tile(np.cos(angles), (8, 1)), np.tile(np.sin(angles), (8, 1))])
     trig = jnp.asarray(trig.astype(np.float32))
     vmem = pl.BlockSpec(memory_space=pltpu.VMEM)
-    hbm = pl.BlockSpec(memory_space=pl.ANY)
     smem = pl.BlockSpec(memory_space=pltpu.SMEM)
     dma = pltpu.SemaphoreType.DMA
-    sems = [dma((2,)), dma((3,)), dma((3,)), dma((15,)), dma((15,)), dma((15,)), dma((15,))]
+    sems = [dma((3,)), dma((3,)), dma((15,)), dma((15,)), dma((15,)), dma((15,))]
     sems += [dma((16,)), dma((8,))] + [dma((8,))] * 4 + [dma((4,))] * 6 + [dma((CHUNKS,))] * 8 + [dma((CHUNKS, 2))] * 2 + [dma((CHUNKS,))] * 2
     sums, evidence = pl.pallas_call(
         kernel,
@@ -539,7 +535,7 @@
             jax.ShapeDtypeStruct((8, 2, pixels), F32),
             jax.ShapeDtypeStruct((local,), F32),
         ),
-        in_specs=[vmem, hbm, hbm, vmem, vmem, smem, smem],
+        in_specs=[vmem, vmem, vmem, vmem, vmem, smem, smem],
         out_specs=(vmem, smem),
         scratch_shapes=[
             pltpu.VMEM((16, 65 * LANES), BF16),
@@ -548,8 +544,7 @@
             pltpu.VMEM((16, LANES), BF16),
             pltpu.VMEM((BLOCKS, 16, LANES), BF16),
             pltpu.VMEM((BLOCKS, 16, HALF), BF16),
-            pltpu.VMEM((2, 128, HALF), BF16),
-            pltpu.VMEM((64, HALF), F32),
+            pltpu.VMEM((128, HALF), BF16),
             pltpu.VMEM((2 * HALF, 128), BF16),
             pltpu.VMEM((64, 128), F32),
             pltpu.VMEM((128, 128), F32),

time: 78 us -> 78 us (level)
  no operation moved by 1% of the time
where the time goes in v16:
time: 78 us; the launch traced here: 77.8 us
  Pallas kernels  73.6 us (94%)
  local copies, waits for them, and re-layouts  3.51 us (4%)
    pallas_call x1, Pallas kernels, per_device(): pl.pallas_call(kernel, out_shape=(jax.ShapeDtypeStruct((8, 2, pixels), F3...  73.6 us
    transpose x1, local copies, waits for them, and re-layouts, per_device(): proj = projections.transpose(1, 0, 2).reshape(128, pixels)  1.96 us

profile of v16, /device:TPU:1, one launch (start us, length us, event | category | flops | bytes accessed | tf_op | source)
XLA Modules:
  0.0 77.8 jit_solution(2335446701367090743)
XLA Ops:
  0.6 0.0 copy-start
  0.6 0.0 copy-start.1
  0.7 0.0 copy-start.2
  0.7 0.0 copy-start.3
  0.7 0.0 copy-start.4
  0.7 0.0 copy-start.5
  0.7 2.0 %copy.9 = bf16[2,64,8320]{2,1,0:T(8,128)(2,1)S(1)} copy(bf16[2,64,8320]{2,0,1:T(2,128)(2,1)} %bitcast.7) | data formatting | bytes 4259840 | tf_op jit(solution)/shard_map/transpose | solution.py:523
  2.7 0.2 copy-done
  2.9 0.0 copy-done.1
  2.9 0.0 copy-done.2
  2.9 0.0 copy-done.3
  2.9 0.0 copy-done.4
  2.9 0.0 copy-done.5
  2.9 73.6 %shard_map.86 = (f32[8,2,8320]{2,1,0:T(2,128)S(1)}, f32[4]{0:T(128)S(1)}) custom-call(bf16[4,2,8320]{2,1,0:T(2,128)(2,1)S(1)} %copy-done.1, bf16[128,8320]{1,0:T(8,128)(2,1)S(1)} %bitcast.4, f32[64,8320]{1,0:T(8,128)S(1)} %copy-done, f32[65,128]{1,0:T(8,128)S(1)} %bitcast.5, f32[16,128]{1,0:T(8,128)S(1)} %copy-done.3, s32[4,2,4]{2,1,0:T(2,128)S(1)} %bitcast.6, ...), custom_call_target="tpu_custom_call" | custom-call | tf_op jit(solution)/shard_map/pallas_call | solution.py:532
  76.5 0.5 copy.12
  77.0 0.8 %copy.13 = f32[8,2,8320]{2,1,0:T(2,128)} copy(f32[8,2,8320]{2,1,0:T(2,128)S(1)} %get-tuple-element.9) | data formatting | bytes 1064960
Async XLA Ops:
  0.6 2.2 %copy-start = (f32[64,8320]{1,0:T(8,128)S(1)}, f32[64,8320]{1,0:T(8,128)}, u32[]{:S(2)}) copy-start(f32[64,8320]{1,0:T(8,128)} %ctf_ref.1) | copy-start | bytes 6389764
  0.6 2.2 %copy-start.1 = (bf16[4,2,8320]{2,1,0:T(2,128)(2,1)S(1)}, bf16[4,2,8320]{2,1,0:T(2,128)(2,1)}, u32[]{:S(2)}) copy-start(bf16[4,2,8320]{2,1,0:T(2,128)(2,1)} %img_ref.1) | copy-start | bytes 399364
  0.7 2.2 %copy-start.2 = (f32[8320]{0:T(1024)S(1)}, f32[8320]{0:T(1024)}, u32[]{:S(2)}) copy-start(f32[8320]{0:T(1024)} %param.10) | copy-start | bytes 99844
  0.7 2.2 %copy-start.3 = (f32[16,128]{1,0:T(8,128)S(1)}, f32[16,128]{1,0:T(8,128)}, u32[]{:S(2)}) copy-start(f32[16,128]{1,0:T(8,128)} %constant.2.clone.trig_ref) | copy-start | bytes 24580
  0.7 2.2 %copy-start.4 = (s32[4,4,2]{1,2,0:T(2,128)S(1)}, s32[4,4,2]{1,2,0:T(2,128)}, u32[]{:S(2)}) copy-start(s32[4,4,2]{1,2,0:T(2,128)} %param.11) | copy-start | bytes 388
  0.7 2.2 %copy-start.5 = (s32[4]{0:T(128)S(1)}, s32[4]{0:T(128)}, u32[]{:S(2)}) copy-start(s32[4]{0:T(128)} %class_ref.1) | copy-start | bytes 52
